TPU v7x, 128 devices: a whole 4x4x4 slice. The times are simulated.
128 devices in a mesh: lat: 8 (over y, core), lon: 16 (over x, z).
Axes of the slice: x: 4, y: 4, z: 4, core: 2. Of those that a mesh axis runs over, the one named last changes fastest.
Arguments:
- state: bfloat16 [64, 1024, 256], P('lat', 'lon'), may hold values from -6 to 6
- background: bfloat16 [64, 1024, 256], P('lat', 'lon'), may hold values from -6 to 6
- conv_in: bfloat16 [3, 3, 256, 256], replicated, may hold values from -0.125 to 0.125
- conv_out: bfloat16 [3, 3, 256, 256], replicated, may hold values from -0.125 to 0.125
- probe: float32 [256], replicated, may hold values from -0.375 to 0.375
- tile_ids: int32 [262144, 1], P(('lat', 'lon')), may hold values from 0 to 127; in each aligned block of 2048 rows (0 to 2047, 2048 to 4095, ...) at most 32 rows name the same one
- cell_taps: int32 [4, 262144], P(None, ('lat', 'lon')), may hold values from 0 to 511
- tap_weights: float32 [4, 262144], P(None, ('lat', 'lon')), may hold values from 0 to 1
- obs_values: float32 [262144], P(('lat', 'lon')), may hold values from -6 to 6
- obs_precision: float32 [262144], P(('lat', 'lon')), may hold values from 0.5 to 2
Outputs:
- grad_state: bfloat16 [64, 1024, 256], P('lat', 'lon')
- innovation: float32 [262144], P(('lat', 'lon'))
Inputs may be any that keep to these rules, and one draw needn't show every extreme that they name: `tile_ids`: among the rows held by one device, no tile is named by more than 32 of them, a bound that some block reaches.
All inputs are finite; a program needn't handle non-finite values.
Results may differ from a plain program's by a relative error of at most 0.006.
Values may be sent and summed in bfloat16 or wider, within the bound.
A program may use at most 128 MiB of HBM per device.

v0:
```python
import jax
import jax.numpy as jnp
from jax import lax
from jax.sharding import PartitionSpec as P


def extended(block, sides, width, periodic):
    for axis, dim in sides:
        count = lax.axis_size(axis)
        forward = [(i, i + 1) for i in range(count - 1)]
        if periodic:
            forward.append((count - 1, 0))
        backward = [(target, source) for source, target in forward]
        low = lax.ppermute(
            lax.slice_in_dim(block, block.shape[dim] - width, None, axis=dim), axis, forward
        )
        high = lax.ppermute(lax.slice_in_dim(block, 0, width, axis=dim), axis, backward)
        block = jnp.concatenate([low, block, high], axis=dim)
    return block


def extend(field, width):
    tall = extended(field, (("lat", 0),), width, False)
    return extended(tall, (("lon", 1),), width, True)


def correlate(grown, kernel, flipped):
    height = grown.shape[0] - 2
    breadth = grown.shape[1] - 2
    chans = grown.shape[2]
    total = jnp.zeros((height * breadth, kernel.shape[3]), jnp.float32)
    for i in range(3):
        window = jnp.concatenate(
            [grown[i : i + height, j : j + breadth] for j in range(3)], axis=2
        ).reshape(height * breadth, 3 * chans)
        if flipped:
            stacked = jnp.concatenate([kernel[2 - i, 2 - j].T for j in range(3)], axis=0)
        else:
            stacked = kernel[i].reshape(3 * chans, kernel.shape[3])
        total = total + jnp.dot(window, stacked, preferred_element_type=jnp.float32)
    return total.reshape(height, breadth, kernel.shape[3])


def slope_of(before):
    sigma = jax.nn.sigmoid(before)
    return sigma * (1.0 + before * (1.0 - sigma))


def indicator(tap_row, cell_count):
    positions = jnp.arange(cell_count, dtype=jnp.int32)
    return (tap_row[:, None] == positions[None, :]).astype(jnp.float32)


def send_out(packed):
    return lax.all_to_all(packed, ("lat", "lon"), split_axis=1, concat_axis=1, tiled=True)


def send_back(packed):
    return lax.all_to_all(packed, ("lat", "lon"), split_axis=1, concat_axis=1, tiled=True)


def on_device(
    state,
    background,
    conv_in,
    conv_out,
    probe,
    tile_ids,
    cell_taps,
    tap_weights,
    obs_values,
    obs_precision,
):
    rows, cols, chans = state.shape
    cell_count = rows * cols
    lat_count = lax.axis_size("lat")
    lon_count = lax.axis_size("lon")
    tiles = lat_count * lon_count
    count = obs_values.shape[0]
    capacity = 2 * count // tiles
    slots = tiles * capacity
    before = correlate(extend(state, 1), conv_in, False)
    hidden = jax.nn.silu(before).astype(jnp.bfloat16)
    mixed = state.astype(jnp.float32) + correlate(extend(hidden, 1), conv_out, False)
    dest = tile_ids[:, 0]
    onehot = (dest[:, None] == jnp.arange(tiles, dtype=jnp.int32)[None, :]).astype(jnp.int32)
    ranks = jnp.cumsum(onehot, axis=0)
    place = dest * capacity + jnp.sum(ranks * onehot, axis=1) - 1
    fields = jnp.concatenate(
        [cell_taps.astype(jnp.float32), tap_weights, obs_values[None, :], obs_precision[None, :]],
        axis=0,
    )
    packed = jnp.zeros((10, slots), jnp.float32).at[:, place].set(fields)
    arrived = send_out(packed)
    scalar = jnp.sum(mixed * probe, axis=-1).reshape(-1)
    taps = arrived[0:4].astype(jnp.int32)
    weights = arrived[4:8]
    predicted = jnp.zeros((slots,), jnp.float32)
    for k in range(4):
        looked = jnp.dot(indicator(taps[k], cell_count), scalar, precision=lax.Precision.HIGHEST)
        predicted = predicted + weights[k] * looked
    residual = arrived[9] * (predicted - arrived[8])
    shares = weights * (arrived[9] * residual)[None, :]
    spread = jnp.zeros((cell_count,), jnp.float32)
    for k in range(4):
        spread = spread + jnp.dot(
            shares[k], indicator(taps[k], cell_count), precision=lax.Precision.HIGHEST
        )
    spread = spread.reshape(rows, cols)
    returned = send_back(residual[None, :])
    innovation = returned[0, place]
    adjoint = (
        mixed - background.astype(jnp.float32) + spread[:, :, None] * probe[None, None, :]
    ).astype(jnp.bfloat16)
    back_hidden = correlate(extend(adjoint, 1), conv_out, True)
    back_before = (back_hidden * slope_of(before)).astype(jnp.bfloat16)
    grad_state = adjoint.astype(jnp.float32) + correlate(extend(back_before, 1), conv_in, True)
    return (grad_state.astype(jnp.bfloat16), innovation)


def solution(mesh):
    in_specs = (
        P("lat", "lon", None),
        P("lat", "lon", None),
        P(),
        P(),
        P(),
        P(("lat", "lon"), None),
        P(None, ("lat", "lon")),
        P(None, ("lat", "lon")),
        P(("lat", "lon")),
        P(("lat", "lon")),
    )
    out_specs = (P("lat", "lon", None), P(("lat", "lon")))
    return jax.shard_map(
        on_device, mesh=mesh, in_specs=in_specs, out_specs=out_specs, check_vma=False
    )
```

profile of v0, /device:TPU:1, one launch (start us, length us, event | category | flops | bytes accessed | tf_op | source)
XLA Modules:
  0.0 168.2 jit_solution(18445499988395505951)
XLA Ops:
  1.4 4.6 %collective-permute-start = (bf16[1,64,256]{2,1,0:T(8,128)(2,1)S(1)}, bf16[1,64,256]{2,1,0:T(8,128)(2,1)S(1)}, u32[]{:S(2)}, u32[]{:S(2)}) collective-permute-start(bf16[1,64,256]{2,1,0:T(8,128)(2,1)S(1)} %get-tuple-element.99), channel_id=1, source_target_pairs={{0,16},{16,32},{32,48},{48,64},{64,80},{80,96},{96,112},{1,17},{17... | collective-permute-start | bytes 98312 | tf_op jit(solution)/shard_map/ppermute | solution.py:14
  6.0 1.9 %collective-permute-start.1 = (bf16[1,64,256]{2,1,0:T(8,128)(2,1)S(1)}, bf16[1,64,256]{2,1,0:T(8,128)(2,1)S(1)}, u32[]{:S(2)}, u32[]{:S(2)}) collective-permute-start(bf16[1,64,256]{2,1,0:T(8,128)(2,1)S(1)} %get-tuple-element.98), channel_id=1, source_target_pairs={{16,0},{32,16},{48,32},{64,48},{80,64},{96,80},{112,96},{17,1},{33... | collective-permute-start | bytes 98312 | tf_op jit(solution)/shard_map/ppermute | solution.py:17
  11.3 1.7 %collective-permute-start.2 = (bf16[10,1,256]{2,1,0:T(2,128)(2,1)S(1)}, bf16[10,1,256]{2,1,0:T(2,128)(2,1)S(1)}, u32[]{:S(2)}, u32[]{:S(2)}) collective-permute-start(bf16[10,1,256]{2,1,0:T(2,128)(2,1)S(1)} %get-tuple-element.78), channel_id=1, source_target_pairs={{0,1},{1,2},{2,3},{3,4},{4,5},{5,6},{6,7},{7,8},{8,9},{9,10},{10,1... | collective-permute-start | bytes 15368 | tf_op jit(solution)/shard_map/ppermute | solution.py:14
  13.0 4.4 %collective-permute-start.3 = (bf16[10,1,256]{2,1,0:T(2,128)(2,1)S(1)}, bf16[10,1,256]{2,1,0:T(2,128)(2,1)S(1)}, u32[]{:S(2)}, u32[]{:S(2)}) collective-permute-start(bf16[10,1,256]{2,1,0:T(2,128)(2,1)S(1)} %get-tuple-element.79), channel_id=1, source_target_pairs={{1,0},{2,1},{3,2},{4,3},{5,4},{6,5},{7,6},{8,7},{9,8},{10,9},{11,1... | collective-permute-start | bytes 15368 | tf_op jit(solution)/shard_map/ppermute | solution.py:17
  20.2 3.9 %collective-permute-start.4 = (bf16[1,64,256]{2,1,0:T(8,128)(2,1)S(1)}, bf16[1,64,256]{2,1,0:T(8,128)(2,1)S(1)}, u32[]{:S(2)}, u32[]{:S(2)}) collective-permute-start(bf16[1,64,256]{2,1,0:T(8,128)(2,1)S(1)} %get-tuple-element.94), channel_id=1, source_target_pairs={{0,16},{16,32},{32,48},{48,64},{64,80},{80,96},{96,112},{1,17},{17... | collective-permute-start | bytes 98312 | tf_op jit(solution)/shard_map/ppermute | solution.py:14
  24.2 1.9 %collective-permute-start.5 = (bf16[1,64,256]{2,1,0:T(8,128)(2,1)S(1)}, bf16[1,64,256]{2,1,0:T(8,128)(2,1)S(1)}, u32[]{:S(2)}, u32[]{:S(2)}) collective-permute-start(bf16[1,64,256]{2,1,0:T(8,128)(2,1)S(1)} %get-tuple-element.93), channel_id=1, source_target_pairs={{16,0},{32,16},{48,32},{64,48},{80,64},{96,80},{112,96},{17,1},{33... | collective-permute-start | bytes 98312 | tf_op jit(solution)/shard_map/ppermute | solution.py:17
  27.6 6.5 %scatter_custom_fusion = f32[10,4096]{0,1:T(8,128)S(1)} fusion(s32[2048]{0:T(1024)S(1)} %bitcast.198, f32[2048,10]{1,0:T(8,128)} %copy.24, f32[]{:T(128)} %constant.7.clone.1), kind=kCustom, calls=%fused_computation.36 | custom fusion | bytes 164352 | tf_op jit(solution)/shard_map/scatter | solution.py:93
  34.0 1.9 %copy.25 = f32[10,128,32]{2,0,1:T(8,128)} copy(f32[10,128,32]{0,2,1:T(8,128)S(1)} %bitcast.164) | data formatting | bytes 327680 | tf_op jit(solution)/shard_map/all_to_all | solution.py:55
  35.9 2.4 %reshape.222 = f32[128,1,320]{2,1,0:T(1,128)} reshape(f32[128,10,32]{2,1,0:T(8,128)} %bitcast.168) | data formatting | bytes 327680
  38.3 9.5 %all-to-all-start = ((f32[128,1,320]{2,1,0:T(1,128)}), f32[128,1,320]{2,1,0:T(1,128)S(1)}, u32[]{:S(2)}, u32[]{:S(2)}) async-start(f32[128,1,320]{2,1,0:T(1,128)} %reshape.222), calls=%async_computation | async-start | bytes 393216 | tf_op jit(solution)/shard_map/all_to_all | solution.py:55
  47.8 1.6 collective-permute-start.6
  49.4 4.2 %collective-permute-start.7 = (bf16[10,1,256]{2,1,0:T(2,128)(2,1)S(1)}, bf16[10,1,256]{2,1,0:T(2,128)(2,1)S(1)}, u32[]{:S(2)}, u32[]{:S(2)}) collective-permute-start(bf16[10,1,256]{2,1,0:T(2,128)(2,1)S(1)} %get-tuple-element.75), channel_id=1, source_target_pairs={{1,0},{2,1},{3,2},{4,3},{5,4},{6,5},{7,6},{8,7},{9,8},{10,9},{11,1... | collective-permute-start | bytes 15368 | tf_op jit(solution)/shard_map/ppermute | solution.py:17
  53.7 1.9 %collective-permute-done.6 = bf16[10,1,256]{2,1,0:T(2,128)(2,1)S(1)} collective-permute-done((bf16[10,1,256]{2,1,0:T(2,128)(2,1)S(1)}, bf16[10,1,256]{2,1,0:T(2,128)(2,1)S(1)}, u32[]{:S(2)}, u32[]{:S(2)}) %collective-permute-start.6) | collective-permute-done | bytes 5152 | tf_op jit(solution)/shard_map/ppermute | solution.py:14
  62.5 3.4 %slice_reduce_fusion.8 = (f32[128,32]{1,0:T(8,128)S(1)}, f32[128,32]{1,0:T(8,128)S(1)}, f32[128,32]{1,0:T(8,128)S(1)}, f32[128,32]{1,0:T(8,128)S(1)}, f32[128,32]{1,0:T(8,128)S(1)}, /*index=5*/f32[128,32]{1,0:T(8,128)S(1)}) fusion(f32[10,128,32]{2,0,1:T(8,128)} %bitcast.170), kind=kLoop, calls=%fused_computation.155 | loop fusion | bytes 196608 | tf_op jit(solution)/shard_map/slice | solution.py:101
  69.1 5.0 %fusion.7 = f32[1,4096]{1,0:T(1,128)} fusion(f32[512,1]{0,1:T(1,128)S(1)} %reshape.139, s32[4096]{0:T(1024)S(1)} %eq.58), kind=kOutput, calls=%fused_computation.13 | convolution fusion | flops 27262976 | bytes 34816 | tf_op jit(solution)/shard_map/dot_general | solution.py:100
  74.1 4.9 %fusion.5 = f32[1,4096]{1,0:T(1,128)} fusion(f32[512,1]{0,1:T(1,128)S(1)} %reshape.139, s32[4096]{0:T(1024)S(1)} %eq.62), kind=kOutput, calls=%fused_computation.10 | convolution fusion | flops 27262976 | bytes 34816 | tf_op jit(solution)/shard_map/dot_general | solution.py:100
  79.1 5.0 %fusion.3 = f32[1,4096]{1,0:T(1,128)} fusion(f32[512,1]{0,1:T(1,128)S(1)} %reshape.139, s32[4096]{0:T(1024)S(1)} %eq.129), kind=kOutput, calls=%fused_computation.7 | convolution fusion | flops 27262976 | bytes 34816 | tf_op jit(solution)/shard_map/dot_general | solution.py:100
  84.2 5.0 %fusion.1 = f32[1,4096]{1,0:T(1,128)} fusion(f32[512,1]{0,1:T(1,128)S(1)} %reshape.139, s32[4096]{0:T(1024)S(1)} %eq.133), kind=kOutput, calls=%fused_computation.4 | convolution fusion | flops 27262976 | bytes 34816 | tf_op jit(solution)/shard_map/dot_general | solution.py:100
  90.6 2.7 %fusion.4 = f32[1,512]{1,0:T(1,128)S(1)} fusion(s32[4096]{0:T(1024)S(1)} %eq.62, f32[4,4096]{1,0:T(4,128)S(1)} %broadcast_multiply_fusion), kind=kOutput, calls=%fused_computation.9 | convolution fusion | flops 27262976 | bytes 34816 | tf_op jit(solution)/shard_map/dot_general | solution.py:106
  93.3 2.7 %fusion.6 = f32[1,512]{1,0:T(1,128)S(1)} fusion(s32[4096]{0:T(1024)S(1)} %eq.58, f32[4,4096]{1,0:T(4,128)S(1)} %broadcast_multiply_fusion), kind=kOutput, calls=%fused_computation.12 | convolution fusion | flops 27262976 | bytes 34816 | tf_op jit(solution)/shard_map/dot_general | solution.py:106
  96.0 2.7 %fusion.2 = f32[1,512]{1,0:T(1,128)S(1)} fusion(s32[4096]{0:T(1024)S(1)} %eq.129, f32[4,4096]{1,0:T(4,128)S(1)} %broadcast_multiply_fusion), kind=kOutput, calls=%fused_computation.6 | convolution fusion | flops 27262976 | bytes 34816 | tf_op jit(solution)/shard_map/dot_general | solution.py:106
  98.8 2.7 %fusion = f32[1,512]{1,0:T(1,128)S(1)} fusion(s32[4096]{0:T(1024)S(1)} %copy-done.10, f32[4,4096]{1,0:T(4,128)S(1)} %broadcast_multiply_fusion), kind=kOutput, calls=%fused_computation.3 | convolution fusion | flops 27262976 | bytes 34816 | tf_op jit(solution)/shard_map/dot_general | solution.py:106
  101.7 3.4 %collective-permute-start.8 = (bf16[1,64,256]{2,1,0:T(8,128)(2,1)S(1)}, bf16[1,64,256]{2,1,0:T(8,128)(2,1)S(1)}, u32[]{:S(2)}, u32[]{:S(2)}) collective-permute-start(bf16[1,64,256]{2,1,0:T(8,128)(2,1)S(1)} %get-tuple-element.89), channel_id=1, source_target_pairs={{0,16},{16,32},{32,48},{48,64},{64,80},{80,96},{96,112},{1,17},{17... | collective-permute-start | bytes 98312 | tf_op jit(solution)/shard_map/ppermute | solution.py:14
  105.2 1.9 %collective-permute-start.9 = (bf16[1,64,256]{2,1,0:T(8,128)(2,1)S(1)}, bf16[1,64,256]{2,1,0:T(8,128)(2,1)S(1)}, u32[]{:S(2)}, u32[]{:S(2)}) collective-permute-start(bf16[1,64,256]{2,1,0:T(8,128)(2,1)S(1)} %get-tuple-element.88), channel_id=1, source_target_pairs={{16,0},{32,16},{48,32},{64,48},{80,64},{96,80},{112,96},{17,1},{33... | collective-permute-start | bytes 98312 | tf_op jit(solution)/shard_map/ppermute | solution.py:17
  107.1 3.3 %collective-permute-done.9 = bf16[1,64,256]{2,1,0:T(8,128)(2,1)S(1)} collective-permute-done((bf16[1,64,256]{2,1,0:T(8,128)(2,1)S(1)}, bf16[1,64,256]{2,1,0:T(8,128)(2,1)S(1)}, u32[]{:S(2)}, u32[]{:S(2)}) %collective-permute-start.9) | collective-permute-done | bytes 32800 | tf_op jit(solution)/shard_map/ppermute | solution.py:17
  110.7 4.7 %collective-permute-start.11 = (bf16[10,1,256]{2,1,0:T(2,128)(2,1)S(1)}, bf16[10,1,256]{2,1,0:T(2,128)(2,1)S(1)}, u32[]{:S(2)}, u32[]{:S(2)}) collective-permute-start(bf16[10,1,256]{2,1,0:T(2,128)(2,1)S(1)} %get-tuple-element.71), channel_id=1, source_target_pairs={{1,0},{2,1},{3,2},{4,3},{5,4},{6,5},{7,6},{8,7},{9,8},{10,9},{11,1... | collective-permute-start | bytes 15368 | tf_op jit(solution)/shard_map/ppermute | solution.py:17
  118.4 3.1 %collective-permute-start.12 = (bf16[1,64,256]{2,1,0:T(8,128)(2,1)S(1)}, bf16[1,64,256]{2,1,0:T(8,128)(2,1)S(1)}, u32[]{:S(2)}, u32[]{:S(2)}) collective-permute-start(bf16[1,64,256]{2,1,0:T(8,128)(2,1)S(1)} %get-tuple-element.84), channel_id=1, source_target_pairs={{0,16},{16,32},{32,48},{48,64},{64,80},{80,96},{96,112},{1,17},{17... | collective-permute-start | bytes 98312 | tf_op jit(solution)/shard_map/ppermute | solution.py:14
  121.5 1.9 %collective-permute-start.13 = (bf16[1,64,256]{2,1,0:T(8,128)(2,1)S(1)}, bf16[1,64,256]{2,1,0:T(8,128)(2,1)S(1)}, u32[]{:S(2)}, u32[]{:S(2)}) collective-permute-start(bf16[1,64,256]{2,1,0:T(8,128)(2,1)S(1)} %get-tuple-element.83), channel_id=1, source_target_pairs={{16,0},{32,16},{48,32},{64,48},{80,64},{96,80},{112,96},{17,1},{33... | collective-permute-start | bytes 98312 | tf_op jit(solution)/shard_map/ppermute | solution.py:17
  124.1 9.4 %all-to-all-start.1 = ((f32[1,128,32]{2,0,1:T(1,128)}), f32[1,128,32]{2,0,1:T(1,128)S(1)}, u32[]{:S(2)}, u32[]{:S(2)}) async-start(f32[1,128,32]{2,0,1:T(1,128)} %bitcast.85), calls=%async_computation.1 | async-start | bytes 131072 | tf_op jit(solution)/shard_map/all_to_all | solution.py:59
  135.1 4.0 %collective-permute-start.15 = (bf16[10,1,256]{2,1,0:T(2,128)(2,1)S(1)}, bf16[10,1,256]{2,1,0:T(2,128)(2,1)S(1)}, u32[]{:S(2)}, u32[]{:S(2)}) collective-permute-start(bf16[10,1,256]{2,1,0:T(2,128)(2,1)S(1)} %get-tuple-element.67), channel_id=1, source_target_pairs={{1,0},{2,1},{3,2},{4,3},{5,4},{6,5},{7,6},{8,7},{9,8},{10,9},{11,1... | collective-permute-start | bytes 15368 | tf_op jit(solution)/shard_map/ppermute | solution.py:17
  139.2 3.7 %all-to-all-done.1 = f32[1,128,32]{2,0,1:T(1,128)S(1)} async-done(((f32[1,128,32]{2,0,1:T(1,128)}), f32[1,128,32]{2,0,1:T(1,128)S(1)}, u32[]{:S(2)}, u32[]{:S(2)}) %all-to-all-start.1) | async-done | bytes 16416 | tf_op jit(solution)/shard_map/all_to_all | solution.py:59
  144.4 21.2 %gather_fusion = f32[2048]{0:T(1024)} fusion(f32[1,4096]{1,0:T(1,128)S(1)} %all_to_all.18, s32[2048]{0:T(1024)S(1)} %bitcast.163), kind=kCustom, calls=%fused_computation | custom fusion | bytes 32768 | tf_op jit(solution)/shard_map/gather | solution.py:111
  (134 shorter events, 29.8 us)
Async XLA Ops:
  1.4 9.2 %collective-permute-start = (bf16[1,64,256]{2,1,0:T(8,128)(2,1)S(1)}, bf16[1,64,256]{2,1,0:T(8,128)(2,1)S(1)}, u32[]{:S(2)}, u32[]{:S(2)}) collective-permute-start(bf16[1,64,256]{2,1,0:T(8,128)(2,1)S(1)} %get-tuple-element.99), channel_id=1, source_target_pairs={{0,16},{16,32},{32,48},{48,64},{64,80},{80,96},{96,112},{1,17},{17... | collective-permute-start | bytes 98312 | tf_op jit(solution)/shard_map/ppermute | solution.py:14
  6.0 5.2 %collective-permute-start.1 = (bf16[1,64,256]{2,1,0:T(8,128)(2,1)S(1)}, bf16[1,64,256]{2,1,0:T(8,128)(2,1)S(1)}, u32[]{:S(2)}, u32[]{:S(2)}) collective-permute-start(bf16[1,64,256]{2,1,0:T(8,128)(2,1)S(1)} %get-tuple-element.98), channel_id=1, source_target_pairs={{16,0},{32,16},{48,32},{64,48},{80,64},{96,80},{112,96},{17,1},{33... | collective-permute-start | bytes 98312 | tf_op jit(solution)/shard_map/ppermute | solution.py:17
  9.2 8.1 %copy-start.2 = (bf16[3,3,256,256]{3,2,1,0:T(8,128)(2,1)S(1)}, bf16[3,3,256,256]{3,2,1,0:T(8,128)(2,1)}, u32[]{:S(2)}) copy-start(bf16[3,3,256,256]{3,2,1,0:T(8,128)(2,1)} %param.12) | copy-start | bytes 3538948
  10.5 6.9 %copy-start.7 = (s32[4,2048]{1,0:T(4,128)S(1)}, s32[4,2048]{1,0:T(4,128)}, u32[]{:S(2)}) copy-start(s32[4,2048]{1,0:T(4,128)} %param.16) | copy-start | bytes 98308
  11.3 7.1 %collective-permute-start.2 = (bf16[10,1,256]{2,1,0:T(2,128)(2,1)S(1)}, bf16[10,1,256]{2,1,0:T(2,128)(2,1)S(1)}, u32[]{:S(2)}, u32[]{:S(2)}) collective-permute-start(bf16[10,1,256]{2,1,0:T(2,128)(2,1)S(1)} %get-tuple-element.78), channel_id=1, source_target_pairs={{0,1},{1,2},{2,3},{3,4},{4,5},{5,6},{6,7},{7,8},{8,9},{9,10},{10,1... | collective-permute-start | bytes 15368 | tf_op jit(solution)/shard_map/ppermute | solution.py:14
  13.0 5.4 %collective-permute-start.3 = (bf16[10,1,256]{2,1,0:T(2,128)(2,1)S(1)}, bf16[10,1,256]{2,1,0:T(2,128)(2,1)S(1)}, u32[]{:S(2)}, u32[]{:S(2)}) collective-permute-start(bf16[10,1,256]{2,1,0:T(2,128)(2,1)S(1)} %get-tuple-element.79), channel_id=1, source_target_pairs={{1,0},{2,1},{3,2},{4,3},{5,4},{6,5},{7,6},{8,7},{9,8},{10,9},{11,1... | collective-permute-start | bytes 15368 | tf_op jit(solution)/shard_map/ppermute | solution.py:17
  19.7 6.5 %copy-start.8 = (f32[4,2048]{1,0:T(4,128)S(1)}, f32[4,2048]{1,0:T(4,128)}, u32[]{:S(2)}) copy-start(f32[4,2048]{1,0:T(4,128)} %param.17) | copy-start | bytes 98308
  19.7 6.5 %copy-start.14 = (f32[2048]{0:T(1024)S(1)}, f32[2048]{0:T(1024)}, u32[]{:S(2)}) copy-start(f32[2048]{0:T(1024)} %param.19) | copy-start | bytes 24580
  19.7 6.5 %copy-start.15 = (f32[2048]{0:T(1024)S(1)}, f32[2048]{0:T(1024)}, u32[]{:S(2)}) copy-start(f32[2048]{0:T(1024)} %param.18) | copy-start | bytes 24580
  20.2 27.5 %collective-permute-start.4 = (bf16[1,64,256]{2,1,0:T(8,128)(2,1)S(1)}, bf16[1,64,256]{2,1,0:T(8,128)(2,1)S(1)}, u32[]{:S(2)}, u32[]{:S(2)}) collective-permute-start(bf16[1,64,256]{2,1,0:T(8,128)(2,1)S(1)} %get-tuple-element.94), channel_id=1, source_target_pairs={{0,16},{16,32},{32,48},{48,64},{64,80},{80,96},{96,112},{1,17},{17... | collective-permute-start | bytes 98312 | tf_op jit(solution)/shard_map/ppermute | solution.py:14
  24.2 23.6 %collective-permute-start.5 = (bf16[1,64,256]{2,1,0:T(8,128)(2,1)S(1)}, bf16[1,64,256]{2,1,0:T(8,128)(2,1)S(1)}, u32[]{:S(2)}, u32[]{:S(2)}) collective-permute-start(bf16[1,64,256]{2,1,0:T(8,128)(2,1)S(1)} %get-tuple-element.93), channel_id=1, source_target_pairs={{16,0},{32,16},{48,32},{64,48},{80,64},{96,80},{112,96},{17,1},{33... | collective-permute-start | bytes 98312 | tf_op jit(solution)/shard_map/ppermute | solution.py:17
  35.9 17.7 %copy-start.1 = (bf16[3,3,256,256]{3,2,1,0:T(8,128)(2,1)S(1)}, bf16[3,3,256,256]{3,2,1,0:T(8,128)(2,1)}, u32[]{:S(2)}) copy-start(bf16[3,3,256,256]{3,2,1,0:T(8,128)(2,1)} %param.13) | copy-start | bytes 3538948
  38.3 20.0 %all-to-all-start = ((f32[128,1,320]{2,1,0:T(1,128)}), f32[128,1,320]{2,1,0:T(1,128)S(1)}, u32[]{:S(2)}, u32[]{:S(2)}) async-start(f32[128,1,320]{2,1,0:T(1,128)} %reshape.222), calls=%async_computation | async-start | bytes 393216 | tf_op jit(solution)/shard_map/all_to_all | solution.py:55
  47.8 7.8 %collective-permute-start.6 = (bf16[10,1,256]{2,1,0:T(2,128)(2,1)S(1)}, bf16[10,1,256]{2,1,0:T(2,128)(2,1)S(1)}, u32[]{:S(2)}, u32[]{:S(2)}) collective-permute-start(bf16[10,1,256]{2,1,0:T(2,128)(2,1)S(1)} %get-tuple-element.74), channel_id=1, source_target_pairs={{0,1},{1,2},{2,3},{3,4},{4,5},{5,6},{6,7},{7,8},{8,9},{9,10},{10,1... | collective-permute-start | bytes 15368 | tf_op jit(solution)/shard_map/ppermute | solution.py:14
  49.4 6.2 %collective-permute-start.7 = (bf16[10,1,256]{2,1,0:T(2,128)(2,1)S(1)}, bf16[10,1,256]{2,1,0:T(2,128)(2,1)S(1)}, u32[]{:S(2)}, u32[]{:S(2)}) collective-permute-start(bf16[10,1,256]{2,1,0:T(2,128)(2,1)S(1)} %get-tuple-element.75), channel_id=1, source_target_pairs={{1,0},{2,1},{3,2},{4,3},{5,4},{6,5},{7,6},{8,7},{9,8},{10,9},{11,1... | collective-permute-start | bytes 15368 | tf_op jit(solution)/shard_map/ppermute | solution.py:17
  74.1 5.0 %copy-start.5 = (s32[128,32]{1,0:T(8,128)S(1)}, s32[128,32]{1,0:T(8,128)}, u32[]{:S(2)}) copy-start(s32[128,32]{1,0:T(8,128)} %get-tuple-element.10) | copy-start | bytes 49156
  84.2 5.5 %copy-start.9 = (s32[4096]{0:T(1024)}, s32[4096]{0:T(1024)S(1)}, u32[]{:S(2)}) copy-start(s32[4096]{0:T(1024)S(1)} %eq.133) | copy-start | bytes 49156
  84.2 5.7 %copy-start.11 = (f32[1,4096]{1,0:T(1,128)S(1)}, f32[1,4096]{1,0:T(1,128)}, u32[]{:S(2)}) copy-start(f32[1,4096]{1,0:T(1,128)} %fusion.7) | copy-start | bytes 49156
  84.2 5.7 %copy-start.12 = (f32[1,4096]{1,0:T(1,128)S(1)}, f32[1,4096]{1,0:T(1,128)}, u32[]{:S(2)}) copy-start(f32[1,4096]{1,0:T(1,128)} %fusion.5) | copy-start | bytes 49156
  84.2 5.7 %copy-start.13 = (f32[1,4096]{1,0:T(1,128)S(1)}, f32[1,4096]{1,0:T(1,128)}, u32[]{:S(2)}) copy-start(f32[1,4096]{1,0:T(1,128)} %fusion.3) | copy-start | bytes 49156
  96.0 2.7 %copy-start.10 = (s32[4096]{0:T(1024)S(1)}, s32[4096]{0:T(1024)}, u32[]{:S(2)}) copy-start(s32[4096]{0:T(1024)} %copy-done.9) | copy-start | bytes 49156
  98.8 2.8 %copy-start.4 = (bf16[8,64,256]{2,1,0:T(8,128)(2,1)S(1)}, bf16[8,64,256]{2,1,0:T(8,128)(2,1)}, u32[]{:S(2)}) copy-start(bf16[8,64,256]{2,1,0:T(8,128)(2,1)} %param.11) | copy-start | bytes 786436
  101.7 5.4 %collective-permute-start.8 = (bf16[1,64,256]{2,1,0:T(8,128)(2,1)S(1)}, bf16[1,64,256]{2,1,0:T(8,128)(2,1)S(1)}, u32[]{:S(2)}, u32[]{:S(2)}) collective-permute-start(bf16[1,64,256]{2,1,0:T(8,128)(2,1)S(1)} %get-tuple-element.89), channel_id=1, source_target_pairs={{0,16},{16,32},{32,48},{48,64},{64,80},{80,96},{96,112},{1,17},{17... | collective-permute-start | bytes 98312 | tf_op jit(solution)/shard_map/ppermute | solution.py:14
  105.2 5.2 %collective-permute-start.9 = (bf16[1,64,256]{2,1,0:T(8,128)(2,1)S(1)}, bf16[1,64,256]{2,1,0:T(8,128)(2,1)S(1)}, u32[]{:S(2)}, u32[]{:S(2)}) collective-permute-start(bf16[1,64,256]{2,1,0:T(8,128)(2,1)S(1)} %get-tuple-element.88), channel_id=1, source_target_pairs={{16,0},{32,16},{48,32},{64,48},{80,64},{96,80},{112,96},{17,1},{33... | collective-permute-start | bytes 98312 | tf_op jit(solution)/shard_map/ppermute | solution.py:17
  110.4 5.9 %collective-permute-start.10 = (bf16[10,1,256]{2,1,0:T(2,128)(2,1)S(1)}, bf16[10,1,256]{2,1,0:T(2,128)(2,1)S(1)}, u32[]{:S(2)}, u32[]{:S(2)}) collective-permute-start(bf16[10,1,256]{2,1,0:T(2,128)(2,1)S(1)} %get-tuple-element.70), channel_id=1, source_target_pairs={{0,1},{1,2},{2,3},{3,4},{4,5},{5,6},{6,7},{7,8},{8,9},{9,10},{10,1... | collective-permute-start | bytes 15368 | tf_op jit(solution)/shard_map/ppermute | solution.py:14
  110.7 5.7 %collective-permute-start.11 = (bf16[10,1,256]{2,1,0:T(2,128)(2,1)S(1)}, bf16[10,1,256]{2,1,0:T(2,128)(2,1)S(1)}, u32[]{:S(2)}, u32[]{:S(2)}) collective-permute-start(bf16[10,1,256]{2,1,0:T(2,128)(2,1)S(1)} %get-tuple-element.71), channel_id=1, source_target_pairs={{1,0},{2,1},{3,2},{4,3},{5,4},{6,5},{7,6},{8,7},{9,8},{10,9},{11,1... | collective-permute-start | bytes 15368 | tf_op jit(solution)/shard_map/ppermute | solution.py:17
  117.8 21.3 %copy-start.3 = (bf16[3,3,256,256]{3,2,1,0:T(8,128)(2,1)S(1)}, bf16[3,3,256,256]{3,2,1,0:T(8,128)(2,1)}, u32[]{:S(2)}) copy-start(bf16[3,3,256,256]{3,2,1,0:T(8,128)(2,1)} %param.12) | copy-start | bytes 3538948
  118.4 15.1 %collective-permute-start.12 = (bf16[1,64,256]{2,1,0:T(8,128)(2,1)S(1)}, bf16[1,64,256]{2,1,0:T(8,128)(2,1)S(1)}, u32[]{:S(2)}, u32[]{:S(2)}) collective-permute-start(bf16[1,64,256]{2,1,0:T(8,128)(2,1)S(1)} %get-tuple-element.84), channel_id=1, source_target_pairs={{0,16},{16,32},{32,48},{48,64},{64,80},{80,96},{96,112},{1,17},{17... | collective-permute-start | bytes 98312 | tf_op jit(solution)/shard_map/ppermute | solution.py:14
  121.5 12.0 %collective-permute-start.13 = (bf16[1,64,256]{2,1,0:T(8,128)(2,1)S(1)}, bf16[1,64,256]{2,1,0:T(8,128)(2,1)S(1)}, u32[]{:S(2)}, u32[]{:S(2)}) collective-permute-start(bf16[1,64,256]{2,1,0:T(8,128)(2,1)S(1)} %get-tuple-element.83), channel_id=1, source_target_pairs={{16,0},{32,16},{48,32},{64,48},{80,64},{96,80},{112,96},{17,1},{33... | collective-permute-start | bytes 98312 | tf_op jit(solution)/shard_map/ppermute | solution.py:17
  124.1 18.8 %all-to-all-start.1 = ((f32[1,128,32]{2,0,1:T(1,128)}), f32[1,128,32]{2,0,1:T(1,128)S(1)}, u32[]{:S(2)}, u32[]{:S(2)}) async-start(f32[1,128,32]{2,0,1:T(1,128)} %bitcast.85), calls=%async_computation.1 | async-start | bytes 131072 | tf_op jit(solution)/shard_map/all_to_all | solution.py:59
  133.5 32.1 %collective-permute-start.14 = (bf16[10,1,256]{2,1,0:T(2,128)(2,1)S(1)}, bf16[10,1,256]{2,1,0:T(2,128)(2,1)S(1)}, u32[]{:S(2)}, u32[]{:S(2)}) collective-permute-start(bf16[10,1,256]{2,1,0:T(2,128)(2,1)S(1)} %get-tuple-element.66), channel_id=1, source_target_pairs={{0,1},{1,2},{2,3},{3,4},{4,5},{5,6},{6,7},{7,8},{8,9},{9,10},{10,1... | collective-permute-start | bytes 15368 | tf_op jit(solution)/shard_map/ppermute | solution.py:14
  135.1 30.5 %collective-permute-start.15 = (bf16[10,1,256]{2,1,0:T(2,128)(2,1)S(1)}, bf16[10,1,256]{2,1,0:T(2,128)(2,1)S(1)}, u32[]{:S(2)}, u32[]{:S(2)}) collective-permute-start(bf16[10,1,256]{2,1,0:T(2,128)(2,1)S(1)} %get-tuple-element.67), channel_id=1, source_target_pairs={{1,0},{2,1},{3,2},{4,3},{5,4},{6,5},{7,6},{8,7},{9,8},{10,9},{11,1... | collective-permute-start | bytes 15368 | tf_op jit(solution)/shard_map/ppermute | solution.py:17
  (3 other events, 2.8 us)
where the time goes:
time: 169 us; the launch traced here: 168 us
  starting transfers between devices  63.8 us (38%)
  local copies, waits for them, and re-layouts  47.5 us (28%)
  matrix products  35.3 us (21%)
  waiting for transfers between devices  11.9 us (7%)
  other arithmetic  8.28 us (5%)
    ppermute x8, starting transfers between devices, extended(): lax.ppermute(lax.slice_in_dim(block, 0, width, axis=dim), axis, backward)  24.9 us
    gather x1, local copies, waits for them, and re-layouts, on_device(): innovation = returned[0, place]  21.2 us
    ppermute x8, starting transfers between devices, extended(): lax.ppermute(lax.slice_in_dim(block, block.shape[dim] - width, None, axis...  20.1 us
    dot_general x4, matrix products, on_device(): jnp.dot(indicator(taps[k], cell_count), scalar, precision=lax.Precision.H...  19.8 us
    dot_general x4, matrix products, on_device(): jnp.dot(shares[k], indicator(taps[k], cell_count), precision=lax.Precisio...  10.8 us
    all_to_all x1, starting transfers between devices, send_out(): lax.all_to_all(packed, ('lat', 'lon'), split_axis=1, concat_axis=1, tiled...  9.46 us
    all_to_all x1, starting transfers between devices, send_back(): lax.all_to_all(packed, ('lat', 'lon'), split_axis=1, concat_axis=1, tiled...  9.35 us
    scatter x1, local copies, waits for them, and re-layouts, on_device(): packed = jnp.zeros((10, slots), jnp.float32).at[:, place].set(fields)  6.46 us
  transfers between devices with their start and end apart: 18, of which 7 were waited for; matrix products, arithmetic and copies ran while one was open for 23% of the time, Pallas kernels for 0%

commit v1 on v0

v1 whole, which is shorter than its diff:
```python
import functools

import jax
import jax.numpy as jnp
from jax import lax
from jax.experimental import pallas as pl
from jax.experimental.pallas import tpu as pltpu
from jax.sharding import PartitionSpec as P

MESH = pl.DeviceIdType.MESH
B16 = jnp.bfloat16
F32 = jnp.float32
I32 = jnp.int32
ROWS, COLS, CH = 8, 64, 256
WIDE = 96
PITCH = 80
LATS, LONS = 8, 16
TILES = LATS * LONS
COUNT = 2048
CAP = 32
NT = (((1,), (1,)), ((), ()))
SIDES = [(a, b) for a in (-1, 0, 1) for b in (-1, 0, 1) if (a, b) != (0, 0)]
CORNERS = [s for s in SIDES if s[1] != 0]


def iota(shape, dim):
    return lax.broadcasted_iota(I32, shape, dim)


def halves(x):
    high = x.astype(B16)
    return high, (x - high.astype(F32)).astype(B16)


def products(field, rows, pitch, weights, flipped, prod):
    count = rows * pitch
    lhs = jnp.concatenate(
        [field[i : i + rows].reshape(count, CH) for i in range(3)], axis=1
    )
    for j in range(3):
        if flipped:
            rhs = jnp.concatenate([weights[2 - i, 2 - j] for i in range(3)], axis=1)
            out = lax.dot_general(lhs, rhs, NT, preferred_element_type=F32)
        else:
            rhs = jnp.concatenate([weights[i, j] for i in range(3)], axis=0)
            out = jnp.dot(lhs, rhs, preferred_element_type=F32)
        prod[j, 0, 0:count] = out[:, :128]
        prod[j, 1, 0:count] = out[:, 128:]


def gathered(prod, start, count):
    parts = [
        prod[0, h, start : start + count]
        + prod[1, h, start + 1 : start + 1 + count]
        + prod[2, h, start + 2 : start + 2 + count]
        for h in range(2)
    ]
    return jnp.concatenate(parts, axis=1)


def pack(field, packs):
    sub = iota((16, CH), 0)
    west = jnp.zeros((16, CH), F32)
    east = jnp.zeros((16, CH), F32)
    for r in range(ROWS):
        here = (sub == 2 * r) | (sub == 2 * r + 1)
        x = field[2 + r, 16:32].astype(F32)
        west = jnp.where(here, x if r == 0 else pltpu.roll(x, 2 * r, 0), west)
        x = field[2 + r, 64:80].astype(F32)
        east = jnp.where(here, x if r == 7 else pltpu.roll(x, (2 * r - 14) % 16, 0), east)
    packs[0] = west.astype(B16)
    packs[1] = east.astype(B16)


def unpack(field, arrived):
    for n, (a, b) in enumerate(CORNERS):
        x = arrived[n].astype(F32)
        for r in {-1: (6, 7), 0: range(8), 1: (0, 1)}[a]:
            row = r + 2 + a * 8
            shift = (14 - 2 * r) % 16 if b < 0 else (-2 * r) % 16
            block = (x if shift == 0 else pltpu.roll(x, shift, 0)).astype(B16)
            if b < 0:
                field[row, 0:16] = block
            else:
                field[row, 80:96] = block


def kernel(
    ids, taps, wts, vals, prec, probe, state, background, conv_in, conv_out,
    grad, innov,
    sx, mx, ax, bg, w1, w2, before, hx, mb, prod, dt, rank_s,
    packs, arrived, sbuf, r1, tbuf, r2, qbuf, q1, qs, q2, zs, zr,
    load_sem, row_sem, pack_sem, s1_sem, s2_sem, z_sem, t1_sem, t2_sem, own_sem,
):
    la = lax.axis_index("lat")
    lo = lax.axis_index("lon")

    def near(a, b):
        return (lax.rem(la + a + LATS, LATS), lax.rem(lo + b + LONS, LONS))

    def send(src, dst, sems, to):
        return pltpu.make_async_remote_copy(
            src_ref=src, dst_ref=dst, send_sem=sems[0], recv_sem=sems[1],
            device_id=to, device_id_type=MESH,
        )

    loads = [
        pltpu.make_async_copy(state, sx.at[2:10, 16:80], load_sem.at[0]),
        pltpu.make_async_copy(conv_in, w1, load_sem.at[1]),
        pltpu.make_async_copy(conv_out, w2, load_sem.at[2]),
        pltpu.make_async_copy(background, bg, load_sem.at[3]),
    ]
    for c in loads:
        c.start()

    partners = [near(k, 0) for k in range(1, LATS)] + [near(0, k) for k in range(1, LONS)]
    partners += [near(a, b) for a in (-1, 1) for b in (-1, 1)]
    barrier = pltpu.get_barrier_semaphore()
    for p in partners:
        pl.semaphore_signal(barrier, inc=1, device_id=p, device_id_type=MESH)

    def halo(field, which):
        copies = [
            send(field.at[2:4, 16:80], field.at[10:12, 16:80],
                 (row_sem.at[which, 0, 0], row_sem.at[which, 0, 1]), near(-1, 0)),
            send(field.at[8:10, 16:80], field.at[0:2, 16:80],
                 (row_sem.at[which, 1, 0], row_sem.at[which, 1, 1]), near(1, 0)),
        ]
        for n, (a, b) in enumerate(CORNERS):
            m = CORNERS.index((-a, -b))
            copies.append(
                send(packs.at[which, 0 if b < 0 else 1], arrived.at[which, m],
                     (pack_sem.at[which, n, 0], pack_sem.at[which, m, 1]), near(a, b))
            )
        return copies

    def clear(field, low, high):
        @pl.when(la == 0)
        def _():
            field[0:low] = jnp.zeros((low,) + field.shape[1:], field.dtype)

        @pl.when(la == LATS - 1)
        def _():
            field[high:] = jnp.zeros((field.shape[0] - high,) + field.shape[1:], field.dtype)

    loads[0].wait()
    pack(sx, packs.at[0])
    pl.semaphore_wait(barrier, len(partners))
    first = halo(sx, 0)
    for c in first:
        c.start()

    upper = jnp.where(iota((128, 128), 0) <= iota((128, 128), 1), 1.0, 0.0).astype(B16)
    carry = jnp.zeros((128, 1), F32)
    ranks = []
    for c in range(16):
        hit = iota((128, 128), 0) == ids[0:1, c * 128 : (c + 1) * 128]
        one = jnp.where(hit, 1.0, 0.0).astype(B16)
        dt[:, c * 128 : (c + 1) * 128] = one
        run = jnp.dot(one, upper, preferred_element_type=F32) + carry
        ranks.append(jnp.sum(jnp.where(hit, run, 0.0), axis=0, keepdims=True) - 1.0)
        carry = run[:, 127:128]
    rank = jnp.concatenate(ranks, axis=1)
    rank_s[...] = rank
    acc = jnp.zeros((128, 512), F32)
    for c in range(8):
        cut = slice(c * 256, (c + 1) * 256)
        own = iota((CAP, 256), 0) == rank[:, cut].astype(I32)
        p = prec[0:1, cut]
        rows = [taps[k : k + 1, cut].astype(F32) - 256.0 for k in range(4)]
        scaled = [wts[k : k + 1, cut] * p for k in range(4)] + [vals[0:1, cut] * p]
        tops = [s.astype(B16).astype(F32) for s in scaled]
        lows = [s - t for s, t in zip(scaled, tops)]
        rows += tops[:4] + lows[:4] + [tops[4], lows[4]]
        spots = [jnp.where(own, r, 0.0).astype(B16) for r in rows]
        spots.append(jnp.zeros((64, 256), B16))
        x = jnp.concatenate(spots, axis=0)
        acc = acc + lax.dot_general(dt[:, cut], x, NT, preferred_element_type=F32)
    sbuf[:, 0:128] = acc[:, 0:128]
    sbuf[:, 128:256] = acc[:, 128:256] + acc[:, 256:384]
    sbuf[:, 256:384] = acc[:, 384:512]
    out1 = []
    for k in range(1, LATS):
        to = lax.rem(la + k, LATS)
        out1.append(
            send(sbuf.at[pl.ds(pl.multiple_of(to * 16, 16), 16)], r1.at[la],
                 (s1_sem.at[k, 0], s1_sem.at[k, 1]), (to, lo))
        )
        out1[-1].start()
    mine = pltpu.make_async_copy(
        sbuf.at[pl.ds(pl.multiple_of(la * 16, 16), 16)], r1.at[la], own_sem.at[0]
    )
    mine.start()

    loads[1].wait()
    for c in first:
        c.wait_recv()
    unpack(sx, arrived.at[0])
    clear(sx, 2, 10)
    products(sx, 10, WIDE, w1, False, prod)
    for r in range(10):
        b = gathered(prod, r * WIDE + 14, PITCH)
        before[r] = b
        hx[r] = (b / (1.0 + jnp.exp(-b))).astype(B16)
    clear(hx, 1, 9)

    mine.wait()
    for c in out1:
        c.wait_recv()
    for t in range(LONS):
        for j in range(LATS):
            tbuf[t, j : j + 1, :] = r1[j, t : t + 1, :]
    out2 = []
    for k in range(1, LONS):
        to = lax.rem(lo + k, LONS)
        out2.append(
            send(tbuf.at[to], r2.at[lo], (s2_sem.at[k, 0], s2_sem.at[k, 1]), (la, to))
        )
        out2[-1].start()
    mine2 = pltpu.make_async_copy(tbuf.at[lo], r2.at[lo], own_sem.at[1])
    mine2.start()

    loads[2].wait()
    loads[3].wait()
    products(hx, 8, PITCH, w2, False, prod)
    pr = probe[...]
    ph, plow = halves(pr)
    sub16 = iota((16, CH), 0)
    readout = jnp.where(
        sub16 == 0, ph.astype(F32), jnp.where(sub16 == 1, plow.astype(F32), 0.0)
    ).astype(B16)
    strips = []
    for r in range(ROWS):
        m = gathered(prod, r * PITCH, COLS) + sx[2 + r, 16:80].astype(F32)
        high, low = halves(m)
        s = lax.dot_general(readout, high, NT, preferred_element_type=F32)
        t = lax.dot_general(readout, low, NT, preferred_element_type=F32)
        strips.append(s[0:1] + s[1:2] + t[0:1])
        d = m - bg[r].astype(F32)
        mb[r] = d
        mx[2 + r, 16:80] = d.astype(B16)
    pack(mx, packs.at[1])
    second = halo(mx, 1)
    for c in second:
        c.start()
    tables = [
        jnp.broadcast_to(jnp.concatenate(strips[2 * q : 2 * q + 2], axis=1), (8, 128))
        for q in range(4)
    ]

    mine2.wait()
    for c in out2:
        c.wait_recv()
    cells, shares = [], []
    for t in range(LONS):
        cell = r2[t, :, 0:128].astype(I32) + 256
        w = r2[t, :, 128:256]
        lane = lax.bitwise_and(cell, 127)
        page = lax.shift_right_logical(cell, 7)
        got = jnp.zeros((8, 128), F32)
        for q in range(4):
            look = jnp.take_along_axis(tables[q], lane, axis=1, mode="promise_in_bounds")
            got = jnp.where(page == q, look, got)
        res = w * got - r2[t, :, 256:384]
        res = res + pltpu.roll(res, 64, 1)
        res = res + pltpu.roll(res, 32, 1)
        qbuf[t] = res
        cells.append(cell)
        shares.append(w * res)
    out3 = []
    for k in range(1, LONS):
        to = lax.rem(lo + k, LONS)
        out3.append(
            send(qbuf.at[to], q1.at[lo], (t1_sem.at[k, 0], t1_sem.at[k, 1]), (la, to))
        )
        out3[-1].start()
    mine3 = pltpu.make_async_copy(qbuf.at[lo], q1.at[lo], own_sem.at[2])
    mine3.start()

    total = jnp.zeros((256, 256), F32)
    for t in range(0, LONS, 2):
        cell = jnp.concatenate(cells[t : t + 2], axis=1)
        share = jnp.concatenate(shares[t : t + 2], axis=1)
        upper_cell = lax.shift_right_logical(cell, 5)
        lower_cell = lax.bitwise_and(cell, 31)
        top = share.astype(B16).astype(F32)
        low = share - top
        tops, lows, marks = [], [], []
        for g in range(8):
            hit = iota((16, 256), 0) == upper_cell[g : g + 1]
            tops.append(jnp.where(hit, top[g : g + 1], 0.0).astype(B16))
            lows.append(jnp.where(hit, low[g : g + 1], 0.0).astype(B16))
            marks.append(
                jnp.where(iota((32, 256), 0) == lower_cell[g : g + 1], 1.0, 0.0).astype(B16)
            )
        lhs = jnp.concatenate(tops + lows, axis=0)
        rhs = jnp.concatenate(marks, axis=0)
        total = total + lax.dot_general(lhs, rhs, NT, preferred_element_type=F32)
    total = total[0:128] + total[128:256]
    total = jnp.where(iota((128, 256), 0) // 16 == iota((128, 256), 1) // 32, total, 0.0)
    fold = total[0:16]
    for g in range(1, 8):
        fold = fold + total[g * 16 : (g + 1) * 16]
    fold = fold[:, 0:128] + fold[:, 128:256]
    fold = fold + pltpu.roll(fold, 64, 1)
    fold = fold + pltpu.roll(fold, 32, 1)
    zs[...] = fold
    out4 = []
    for n, (a, b) in enumerate(SIDES):
        m = SIDES.index((-a, -b))
        out4.append(send(zs, zr.at[m], (z_sem.at[n, 0], z_sem.at[m, 1]), near(a, b)))
        out4[-1].start()

    group = iota((16, 128), 1) // 32
    base = jnp.where(iota((128, CH), 0) // 64 == 0, ph.astype(F32), plow.astype(F32)).astype(B16)
    sub = iota((16, 128), 0)
    spot = lax.bitwise_and(iota((16, 128), 1), 31)
    marks = [spot == sub, spot == sub + 16]

    def parted(z):
        top = z.astype(B16).astype(F32)
        return jnp.where(lax.bitwise_and(group, 1) == 0, top, z - top)

    def outer(blocks):
        lhs = jnp.concatenate(
            [
                jnp.where(marks[c % 2], z[2 * r + c // 2 : 2 * r + c // 2 + 1], 0.0).astype(B16)
                for z, r, c in blocks
            ],
            axis=0,
        )
        return jnp.dot(lhs, base, preferred_element_type=F32)

    center = parted(fold)
    local = outer([(center, r, c) for r in range(ROWS) for c in range(4)])
    for r in range(ROWS):
        ax[2 + r, 16:80] = (mb[r] + local[r * 64 : (r + 1) * 64]).astype(B16)
    for c in second:
        c.wait_recv()
    unpack(mx, arrived.at[1])
    for c in out4:
        c.wait_recv()
    around = {s: parted(zr[n]) for n, s in enumerate(SIDES)}
    for a, rows in ((-1, (6, 7)), (1, (0, 1))):
        piece = outer([(around[a, 0], r, c) for r in rows for c in range(4)])
        for n, r in enumerate(rows):
            row = r + 2 + a * 8
            ax[row, 16:80] = (
                mx[row, 16:80].astype(F32) + piece[n * 64 : (n + 1) * 64]
            ).astype(B16)
    for b, c, at in ((-1, 3, 0), (1, 0, 80)):
        spots = [(a, r) for a, rows in ((-1, (6, 7)), (0, range(8)), (1, (0, 1))) for r in rows]
        piece = outer([(around[a, b], r, c) for a, r in spots])
        for n, (a, r) in enumerate(spots):
            row = r + 2 + a * 8
            ax[row, at : at + 16] = (
                mx[row, at : at + 16].astype(F32) + piece[n * 16 : (n + 1) * 16]
            ).astype(B16)
    clear(ax, 2, 10)

    mine3.wait()
    for c in out3:
        c.wait_recv()
    for j in range(LATS):
        for t in range(LONS):
            qs[j, t : t + 1, :] = q1[t, j : j + 1, :]
    out5 = []
    for k in range(1, LATS):
        to = lax.rem(la + k, LATS)
        out5.append(
            send(qs.at[to], q2.at[la], (t2_sem.at[k, 0], t2_sem.at[k, 1]), (to, lo))
        )
        out5[-1].start()
    mine5 = pltpu.make_async_copy(qs.at[la], q2.at[la], own_sem.at[3])
    mine5.start()

    products(ax, 10, WIDE, w2, True, prod)
    for r in range(10):
        x = before[r]
        sigma = 1.0 / (1.0 + jnp.exp(-x))
        y = gathered(prod, r * WIDE + 14, PITCH) * sigma * (1.0 + x * (1.0 - sigma))
        hx[r] = y.astype(B16)
    clear(hx, 1, 9)
    products(hx, 8, PITCH, w1, True, prod)
    for r in range(ROWS):
        y = gathered(prod, r * PITCH, COLS) + ax[2 + r, 16:80].astype(F32)
        grad[r] = y.astype(B16)

    mine5.wait()
    for c in out5:
        c.wait_recv()
    back = q2[...].reshape(TILES, 128).T[0:CAP]
    one = back.astype(B16)
    rest = back - one.astype(F32)
    two = rest.astype(B16)
    three = (rest - two.astype(F32)).astype(B16)
    lhs = jnp.concatenate([one, two, three], axis=0)
    for c in range(4):
        cut = slice(c * 512, (c + 1) * 512)
        got = jnp.dot(lhs, dt[:, cut], preferred_element_type=F32)
        got = got[0:32] + got[32:64] + got[64:96]
        own = iota((CAP, 512), 0) == rank_s[0:1, cut].astype(I32)
        innov[0:1, cut] = jnp.sum(jnp.where(own, got, 0.0), axis=0, keepdims=True)

    for c in first + out1 + out2 + second + out3 + out4 + out5:
        c.wait_send()


def on_device(
    state, background, conv_in, conv_out, probe,
    tile_ids, cell_taps, tap_weights, obs_values, obs_precision,
):
    vmem = pl.BlockSpec(memory_space=pltpu.VMEM)
    hbm = pl.BlockSpec(memory_space=pl.ANY)
    dma = pltpu.SemaphoreType.DMA
    wide = pltpu.VMEM((12, WIDE, CH), B16)
    kshape = (3, 3, CH, CH)
    grad, innov = pl.pallas_call(
        kernel,
        out_shape=(
            jax.ShapeDtypeStruct((ROWS, COLS, CH), B16),
            jax.ShapeDtypeStruct((1, COUNT), F32),
        ),
        in_specs=[vmem] * 6 + [hbm] * 4,
        out_specs=(vmem, vmem),
        scratch_shapes=[
            wide, wide, wide,
            pltpu.VMEM((ROWS, COLS, CH), B16),
            pltpu.VMEM(kshape, B16),
            pltpu.VMEM(kshape, B16),
            pltpu.VMEM((10, PITCH, CH), F32),
            pltpu.VMEM((10, PITCH, CH), B16),
            pltpu.VMEM((ROWS, COLS, CH), F32),
            pltpu.VMEM((3, 2, 10 * WIDE + 64, 128), F32),
            pltpu.VMEM((TILES, COUNT), B16),
            pltpu.VMEM((1, COUNT), F32),
            pltpu.VMEM((2, 2, 16, CH), B16),
            pltpu.VMEM((2, len(CORNERS), 16, CH), B16),
            pltpu.VMEM((TILES, 384), F32),
            pltpu.VMEM((LATS, LONS, 384), F32),
            pltpu.VMEM((LONS, LATS, 384), F32),
            pltpu.VMEM((LONS, LATS, 384), F32),
            pltpu.VMEM((LONS, LATS, 128), F32),
            pltpu.VMEM((LONS, LATS, 128), F32),
            pltpu.VMEM((LATS, LONS, 128), F32),
            pltpu.VMEM((LATS, LONS, 128), F32),
            pltpu.VMEM((16, 128), F32),
            pltpu.VMEM((len(SIDES), 16, 128), F32),
            dma((4,)),
            dma((2, 2, 2)),
            dma((2, len(CORNERS), 2)),
            dma((LATS, 2)),
            dma((LONS, 2)),
            dma((len(SIDES), 2)),
            dma((LONS, 2)),
            dma((LATS, 2)),
            dma((4,)),
        ],
        compiler_params=pltpu.CompilerParams(
            collective_id=0, has_side_effects=True, vmem_limit_bytes=56 * 2**20
        ),
    )(
        tile_ids.reshape(1, COUNT),
        cell_taps,
        tap_weights,
        obs_values.reshape(1, COUNT),
        obs_precision.reshape(1, COUNT),
        probe.reshape(1, CH),
        state,
        background,
        conv_in,
        conv_out,
    )
    return grad, innov.reshape(COUNT)


def solution(mesh):
    in_specs = (
        P("lat", "lon", None),
        P("lat", "lon", None),
        P(),
        P(),
        P(),
        P(("lat", "lon"), None),
        P(None, ("lat", "lon")),
        P(None, ("lat", "lon")),
        P(("lat", "lon")),
        P(("lat", "lon")),
    )
    out_specs = (P("lat", "lon", None), P(("lat", "lon")))
    return jax.shard_map(
        on_device, mesh=mesh, in_specs=in_specs, out_specs=out_specs, check_vma=False
    )
```

time: 169 us -> 38.3 us (0.23)
  starting transfers between devices: 63.8 us -> 0 us
  local copies, waits for them, and re-layouts: 47.5 us -> 2.96 us
  matrix products: 35.3 us -> 0 us
  Pallas kernels: 0 us -> 34.4 us
  waiting for transfers between devices: 11.9 us -> 0 us
  other arithmetic: 8.28 us -> 0 us
    ppermute x16 -> x0, starting transfers between devices: 45 us -> none  [the longest x8 24.9 us: extended(): lax.ppermute(lax.slice_in_dim(block, 0, width, axis=dim), axis, backward)]
    dot_general x20 -> x0, matrix products: 35.3 us -> none  [the longest x4 19.8 us: on_device(): jnp.dot(indicator(taps[k], cell_count), scalar, precision=lax.Precision.H...]
    pallas_call x0 -> x1, Pallas kernels: none -> 34.4 us  [on_device(): pl.pallas_call(kernel, out_shape=(jax.ShapeDtypeStruct((ROWS, COLS, CH),...]
    gather x1 -> x0, local copies, waits for them, and re-layouts: 21.2 us -> none  [on_device(): innovation = returned[0, place]]
    all_to_all x2 -> x0, starting transfers between devices: 18.8 us -> none  [the longest x1 9.46 us: send_out(): lax.all_to_all(packed, ('lat', 'lon'), split_axis=1, concat_axis=1, tiled...]
    ppermute x16 -> x0, waiting for transfers between devices: 7.69 us -> none  [the longest x8 3.9 us: extended(): lax.ppermute(lax.slice_in_dim(block, 0, width, axis=dim), axis, backward)]
    slice x16 -> x0, local copies, waits for them, and re-layouts: 6.49 us -> none  [the longest x1 3.44 us: on_device(): predicted = predicted + weights[k] * looked]
    scatter x1 -> x0, local copies, waits for them, and re-layouts: 6.46 us -> none  [on_device(): packed = jnp.zeros((10, slots), jnp.float32).at[:, place].set(fields)]
  transfers between devices with their start and end apart: 18 -> 0, of which waited for: 7 -> 0; matrix products, arithmetic and copies ran while one was open for 23% -> 0% of each run, Pallas kernels for 0% -> 0%
where the time goes in v1:
time: 38.3 us; the launch traced here: 38 us
  Pallas kernels  34.4 us (90%)
  local copies, waits for them, and re-layouts  2.96 us (8%)
  between operations  0.64 us (2%)
    pallas_call x1, Pallas kernels, on_device(): pl.pallas_call(kernel, out_shape=(jax.ShapeDtypeStruct((ROWS, COLS, CH),...  34.4 us
    unnamed x2, local copies, waits for them, and re-layouts  2.96 us

profile of v1, /device:TPU:1, one launch (start us, length us, event | category | flops | bytes accessed | tf_op | source)
XLA Modules:
  0.0 38.0 jit_solution(12457606338708136330)
XLA Ops:
  0.6 34.4 %shard_map.113 = (bf16[8,64,256]{2,1,0:T(8,128)(2,1)}, f32[1,2048]{1,0:T(1,128)}) custom-call(s32[1,2048]{1,0:T(1,128)} %bitcast.5, s32[4,2048]{1,0:T(4,128)} %taps.1, f32[4,2048]{1,0:T(4,128)} %wts.1, f32[1,2048]{1,0:T(1,128)} %bitcast.6, f32[1,2048]{1,0:T(1,128)} %bitcast.7, f32[1,256]{1,0:T(1,128)} %bitcast.9, bf16[8,64,256]{2,1,0:T(8,128)(2,1)} %state.1, ...), custom_call_target="tpu_custom_call" | custom-call | tf_op jit(solution)/shard_map/pallas_call | solution.py:418
  35.1 1.7 %copy.14 = bf16[8,64,256]{2,1,0:T(8,128)(2,1)} copy(bf16[8,64,256]{2,1,0:T(8,128)(2,1)} %get-tuple-element.8) | data formatting | bytes 524288
  36.7 1.3 %copy.15 = f32[2048]{0:T(1024)} copy(f32[2048]{0:T(1024)} %bitcast.8) | data formatting | bytes 16384

commit v2 on v1

--- a/solution.py
+++ b/solution.py
@@ -86,11 +86,11 @@
 
 
 def kernel(
-    ids, taps, wts, vals, prec, probe, state, background, conv_in, conv_out,
+    ids_in, taps_in, wts_in, vals_in, prec_in, probe_in, state, background, conv_in, conv_out,
     grad, innov,
-    sx, mx, ax, bg, w1, w2, before, hx, mb, prod, dt, rank_s,
-    packs, arrived, sbuf, r1, tbuf, r2, qbuf, q1, qs, q2, zs, zr,
-    load_sem, row_sem, pack_sem, s1_sem, s2_sem, z_sem, t1_sem, t2_sem, own_sem,
+    ids, taps, wts, vals, prec, probe, sx, mx, ax, bg, w1, w2, before, hx, mb, prod, dt, rank_s,
+    packs, arrived, sbuf, r2, qbuf, q2, zs, zr,
+    load_sem, row_sem, pack_sem, out_sem, back_sem, z_sem, own_sem,
 ):
     la = lax.axis_index("lat")
     lo = lax.axis_index("lon")
@@ -104,20 +104,39 @@
             device_id=to, device_id_type=MESH,
         )
 
-    loads = [
-        pltpu.make_async_copy(state, sx.at[2:10, 16:80], load_sem.at[0]),
-        pltpu.make_async_copy(conv_in, w1, load_sem.at[1]),
-        pltpu.make_async_copy(conv_out, w2, load_sem.at[2]),
-        pltpu.make_async_copy(background, bg, load_sem.at[3]),
-    ]
+    me = la * LONS + lo
+    barrier = pltpu.get_barrier_semaphore()
+
+    def place(k):
+        t = lax.rem(me + k, TILES)
+        return t, (t // LONS, lax.rem(t, LONS))
+
+    def greet(k, c):
+        pl.semaphore_signal(barrier, inc=1, device_id=place(k)[1], device_id_type=MESH)
+        return c
+
+    lax.fori_loop(1, TILES, greet, 0)
+    ins = [(ids_in, ids), (taps_in, taps), (wts_in, wts), (vals_in, vals), (prec_in, prec)]
+    ins += [(state, sx.at[2:10, 16:80]), (conv_in, w1), (conv_out, w2), (background, bg)]
+    ins += [(probe_in, probe)]
+    loads = [pltpu.make_async_copy(a, b, load_sem.at[n]) for n, (a, b) in enumerate(ins)]
     for c in loads:
         c.start()
 
-    partners = [near(k, 0) for k in range(1, LATS)] + [near(0, k) for k in range(1, LONS)]
-    partners += [near(a, b) for a in (-1, 1) for b in (-1, 1)]
-    barrier = pltpu.get_barrier_semaphore()
-    for p in partners:
-        pl.semaphore_signal(barrier, inc=1, device_id=p, device_id_type=MESH)
+    def scatter(src, dst, sems):
+        def one(k, c):
+            t, to = place(k)
+            send(src.at[t], dst.at[me], (sems.at[0], sems.at[1]), to).start()
+            return c
+
+        lax.fori_loop(1, TILES, one, 0)
+        own = pltpu.make_async_copy(src.at[me], dst.at[me], own_sem.at[0])
+        own.start()
+        own.wait()
+
+    def settle(src, dst, sem):
+        some = slice(0, TILES - 1)
+        pltpu.make_async_copy(src.at[some], dst.at[some], sem).wait()
 
     def halo(field, which):
         copies = [
@@ -143,13 +162,8 @@
         def _():
             field[high:] = jnp.zeros((field.shape[0] - high,) + field.shape[1:], field.dtype)
 
-    loads[0].wait()
-    pack(sx, packs.at[0])
-    pl.semaphore_wait(barrier, len(partners))
-    first = halo(sx, 0)
-    for c in first:
-        c.start()
-
+    for c in loads[:5]:
+        c.wait()
     upper = jnp.where(iota((128, 128), 0) <= iota((128, 128), 1), 1.0, 0.0).astype(B16)
     carry = jnp.zeros((128, 1), F32)
     ranks = []
@@ -176,23 +190,19 @@
         spots.append(jnp.zeros((64, 256), B16))
         x = jnp.concatenate(spots, axis=0)
         acc = acc + lax.dot_general(dt[:, cut], x, NT, preferred_element_type=F32)
-    sbuf[:, 0:128] = acc[:, 0:128]
-    sbuf[:, 128:256] = acc[:, 128:256] + acc[:, 256:384]
-    sbuf[:, 256:384] = acc[:, 384:512]
-    out1 = []
-    for k in range(1, LATS):
-        to = lax.rem(la + k, LATS)
-        out1.append(
-            send(sbuf.at[pl.ds(pl.multiple_of(to * 16, 16), 16)], r1.at[la],
-                 (s1_sem.at[k, 0], s1_sem.at[k, 1]), (to, lo))
-        )
-        out1[-1].start()
-    mine = pltpu.make_async_copy(
-        sbuf.at[pl.ds(pl.multiple_of(la * 16, 16), 16)], r1.at[la], own_sem.at[0]
-    )
-    mine.start()
-
-    loads[1].wait()
+    sbuf[:, 0, 0:128] = acc[:, 0:128]
+    sbuf[:, 0, 128:256] = acc[:, 128:256] + acc[:, 256:384]
+    sbuf[:, 0, 256:384] = acc[:, 384:512]
+
+    loads[5].wait()
+    pack(sx, packs.at[0])
+    pl.semaphore_wait(barrier, TILES - 1)
+    first = halo(sx, 0)
+    for c in first:
+        c.start()
+    scatter(sbuf, r2, out_sem)
+
+    loads[6].wait()
     for c in first:
         c.wait_recv()
     unpack(sx, arrived.at[0])
@@ -204,24 +214,8 @@
         hx[r] = (b / (1.0 + jnp.exp(-b))).astype(B16)
     clear(hx, 1, 9)
 
-    mine.wait()
-    for c in out1:
-        c.wait_recv()
-    for t in range(LONS):
-        for j in range(LATS):
-            tbuf[t, j : j + 1, :] = r1[j, t : t + 1, :]
-    out2 = []
-    for k in range(1, LONS):
-        to = lax.rem(lo + k, LONS)
-        out2.append(
-            send(tbuf.at[to], r2.at[lo], (s2_sem.at[k, 0], s2_sem.at[k, 1]), (la, to))
-        )
-        out2[-1].start()
-    mine2 = pltpu.make_async_copy(tbuf.at[lo], r2.at[lo], own_sem.at[1])
-    mine2.start()
-
-    loads[2].wait()
-    loads[3].wait()
+    for c in loads[7:]:
+        c.wait()
     products(hx, 8, PITCH, w2, False, prod)
     pr = probe[...]
     ph, plow = halves(pr)
@@ -248,37 +242,27 @@
         for q in range(4)
     ]
 
-    mine2.wait()
-    for c in out2:
-        c.wait_recv()
+    settle(sbuf, r2, out_sem.at[1])
     cells, shares = [], []
-    for t in range(LONS):
-        cell = r2[t, :, 0:128].astype(I32) + 256
-        w = r2[t, :, 128:256]
+    for t in range(TILES // 8):
+        own = slice(8 * t, 8 * t + 8)
+        cell = r2[own, 0, 0:128].astype(I32) + 256
+        w = r2[own, 0, 128:256]
         lane = lax.bitwise_and(cell, 127)
         page = lax.shift_right_logical(cell, 7)
         got = jnp.zeros((8, 128), F32)
         for q in range(4):
             look = jnp.take_along_axis(tables[q], lane, axis=1, mode="promise_in_bounds")
             got = jnp.where(page == q, look, got)
-        res = w * got - r2[t, :, 256:384]
+        res = w * got - r2[own, 0, 256:384]
         res = res + pltpu.roll(res, 64, 1)
         res = res + pltpu.roll(res, 32, 1)
-        qbuf[t] = res
+        qbuf[own, 0, :] = res
         cells.append(cell)
         shares.append(w * res)
-    out3 = []
-    for k in range(1, LONS):
-        to = lax.rem(lo + k, LONS)
-        out3.append(
-            send(qbuf.at[to], q1.at[lo], (t1_sem.at[k, 0], t1_sem.at[k, 1]), (la, to))
-        )
-        out3[-1].start()
-    mine3 = pltpu.make_async_copy(qbuf.at[lo], q1.at[lo], own_sem.at[2])
-    mine3.start()
 
     total = jnp.zeros((256, 256), F32)
-    for t in range(0, LONS, 2):
+    for t in range(0, TILES // 8, 2):
         cell = jnp.concatenate(cells[t : t + 2], axis=1)
         share = jnp.concatenate(shares[t : t + 2], axis=1)
         upper_cell = lax.shift_right_logical(cell, 5)
@@ -311,6 +295,8 @@
         out4.append(send(zs, zr.at[m], (z_sem.at[n, 0], z_sem.at[m, 1]), near(a, b)))
         out4[-1].start()
 
+    scatter(qbuf, q2, back_sem)
+
     group = iota((16, 128), 1) // 32
     base = jnp.where(iota((128, CH), 0) // 64 == 0, ph.astype(F32), plow.astype(F32)).astype(B16)
     sub = iota((16, 128), 0)
@@ -358,22 +344,6 @@
             ).astype(B16)
     clear(ax, 2, 10)
 
-    mine3.wait()
-    for c in out3:
-        c.wait_recv()
-    for j in range(LATS):
-        for t in range(LONS):
-            qs[j, t : t + 1, :] = q1[t, j : j + 1, :]
-    out5 = []
-    for k in range(1, LATS):
-        to = lax.rem(la + k, LATS)
-        out5.append(
-            send(qs.at[to], q2.at[la], (t2_sem.at[k, 0], t2_sem.at[k, 1]), (to, lo))
-        )
-        out5[-1].start()
-    mine5 = pltpu.make_async_copy(qs.at[la], q2.at[la], own_sem.at[3])
-    mine5.start()
-
     products(ax, 10, WIDE, w2, True, prod)
     for r in range(10):
         x = before[r]
@@ -386,10 +356,8 @@
         y = gathered(prod, r * PITCH, COLS) + ax[2 + r, 16:80].astype(F32)
         grad[r] = y.astype(B16)
 
-    mine5.wait()
-    for c in out5:
-        c.wait_recv()
-    back = q2[...].reshape(TILES, 128).T[0:CAP]
+    settle(qbuf, q2, back_sem.at[1])
+    back = q2[:, 0, :].T[0:CAP]
     one = back.astype(B16)
     rest = back - one.astype(F32)
     two = rest.astype(B16)
@@ -402,8 +370,10 @@
         own = iota((CAP, 512), 0) == rank_s[0:1, cut].astype(I32)
         innov[0:1, cut] = jnp.sum(jnp.where(own, got, 0.0), axis=0, keepdims=True)
 
-    for c in first + out1 + out2 + second + out3 + out4 + out5:
+    for c in first + second + out4:
         c.wait_send()
+    settle(sbuf, r2, out_sem.at[0])
+    settle(qbuf, q2, back_sem.at[0])
 
 
 def on_device(
@@ -421,9 +391,15 @@
             jax.ShapeDtypeStruct((ROWS, COLS, CH), B16),
             jax.ShapeDtypeStruct((1, COUNT), F32),
         ),
-        in_specs=[vmem] * 6 + [hbm] * 4,
+        in_specs=[hbm] * 10,
         out_specs=(vmem, vmem),
         scratch_shapes=[
+            pltpu.VMEM((1, COUNT), I32),
+            pltpu.VMEM((4, COUNT), I32),
+            pltpu.VMEM((4, COUNT), F32),
+            pltpu.VMEM((1, COUNT), F32),
+            pltpu.VMEM((1, COUNT), F32),
+            pltpu.VMEM((1, CH), F32),
             wide, wide, wide,
             pltpu.VMEM((ROWS, COLS, CH), B16),
             pltpu.VMEM(kshape, B16),
@@ -436,25 +412,19 @@
             pltpu.VMEM((1, COUNT), F32),
             pltpu.VMEM((2, 2, 16, CH), B16),
             pltpu.VMEM((2, len(CORNERS), 16, CH), B16),
-            pltpu.VMEM((TILES, 384), F32),
-            pltpu.VMEM((LATS, LONS, 384), F32),
-            pltpu.VMEM((LONS, LATS, 384), F32),
-            pltpu.VMEM((LONS, LATS, 384), F32),
-            pltpu.VMEM((LONS, LATS, 128), F32),
-            pltpu.VMEM((LONS, LATS, 128), F32),
-            pltpu.VMEM((LATS, LONS, 128), F32),
-            pltpu.VMEM((LATS, LONS, 128), F32),
+            pltpu.VMEM((TILES, 1, 384), F32),
+            pltpu.VMEM((TILES, 1, 384), F32),
+            pltpu.VMEM((TILES, 1, 128), F32),
+            pltpu.VMEM((TILES, 1, 128), F32),
             pltpu.VMEM((16, 128), F32),
             pltpu.VMEM((len(SIDES), 16, 128), F32),
-            dma((4,)),
+            dma((10,)),
             dma((2, 2, 2)),
             dma((2, len(CORNERS), 2)),
-            dma((LATS, 2)),
-            dma((LONS, 2)),
+            dma((2,)),
+            dma((2,)),
             dma((len(SIDES), 2)),
-            dma((LONS, 2)),
-            dma((LATS, 2)),
-            dma((4,)),
+            dma((1,)),
         ],
         compiler_params=pltpu.CompilerParams(
             collective_id=0, has_side_effects=True, vmem_limit_bytes=56 * 2**20

time: 38.3 us -> 34.5 us (0.901)
  Pallas kernels: 34.4 us -> 30.7 us
    pallas_call x1, Pallas kernels: 34.4 us -> 30.7 us  [on_device(): pl.pallas_call(kernel, out_shape=(jax.ShapeDtypeStruct((ROWS, COLS, CH),...]
where the time goes in v2:
time: 34.5 us; the launch traced here: 34.3 us
  Pallas kernels  30.7 us (89%)
  local copies, waits for them, and re-layouts  2.96 us (9%)
  between operations  0.64 us (2%)
    pallas_call x1, Pallas kernels, on_device(): pl.pallas_call(kernel, out_shape=(jax.ShapeDtypeStruct((ROWS, COLS, CH),...  30.7 us
    unnamed x2, local copies, waits for them, and re-layouts  2.96 us

profile of v2, /device:TPU:1, one launch (start us, length us, event | category | flops | bytes accessed | tf_op | source)
XLA Modules:
  0.0 34.3 jit_solution(15872825278249293893)
XLA Ops:
  0.6 30.7 %shard_map.113 = (bf16[8,64,256]{2,1,0:T(8,128)(2,1)}, f32[1,2048]{1,0:T(1,128)}) custom-call(s32[1,2048]{1,0:T(1,128)} %bitcast.5, s32[4,2048]{1,0:T(4,128)} %taps_in.1, f32[4,2048]{1,0:T(4,128)} %wts_in.1, f32[1,2048]{1,0:T(1,128)} %bitcast.6, f32[1,2048]{1,0:T(1,128)} %bitcast.7, f32[1,256]{1,0:T(1,128)} %bitcast.9, bf16[8,64,256]{2,1,0:T(8,128)(2,1)} %state.1, ...), custom_call_target="tpu_custom_call" | custom-call | tf_op jit(solution)/shard_map/pallas_call | solution.py:388
  31.3 1.7 %copy.14 = bf16[8,64,256]{2,1,0:T(8,128)(2,1)} copy(bf16[8,64,256]{2,1,0:T(8,128)(2,1)} %get-tuple-element.8) | data formatting | bytes 524288
  33.0 1.3 %copy.15 = f32[2048]{0:T(1024)} copy(f32[2048]{0:T(1024)} %bitcast.8) | data formatting | bytes 16384

commit v3 on v2

--- a/solution.py
+++ b/solution.py
@@ -23,6 +23,15 @@
 CORNERS = [s for s in SIDES if s[1] != 0]
 
 
+def hops(a, b):
+    y, x, z = a // 2, b // 4, b % 4
+    return min(y, 4 - y) + min(x, 4 - x) + min(z, 4 - z)
+
+
+OTHERS = [(a, b) for a in range(LATS) for b in range(LONS) if (a, b) != (0, 0)]
+OTHERS.sort(key=lambda o: -hops(*o))
+
+
 def iota(shape, dim):
     return lax.broadcasted_iota(I32, shape, dim)
 
@@ -96,7 +105,7 @@
     lo = lax.axis_index("lon")
 
     def near(a, b):
-        return (lax.rem(la + a + LATS, LATS), lax.rem(lo + b + LONS, LONS))
+        return place(a, b)[1]
 
     def send(src, dst, sems, to):
         return pltpu.make_async_remote_copy(
@@ -107,36 +116,30 @@
     me = la * LONS + lo
     barrier = pltpu.get_barrier_semaphore()
 
-    def place(k):
-        t = lax.rem(me + k, TILES)
-        return t, (t // LONS, lax.rem(t, LONS))
-
-    def greet(k, c):
-        pl.semaphore_signal(barrier, inc=1, device_id=place(k)[1], device_id_type=MESH)
-        return c
-
-    lax.fori_loop(1, TILES, greet, 0)
-    ins = [(ids_in, ids), (taps_in, taps), (wts_in, wts), (vals_in, vals), (prec_in, prec)]
+    def place(a, b):
+        to = (lax.bitwise_and(la + a, LATS - 1), lax.bitwise_and(lo + b, LONS - 1))
+        return to[0] * LONS + to[1], to
+
+    ins = [(ids_in, ids), (prec_in, prec), (taps_in, taps), (wts_in, wts), (vals_in, vals)]
     ins += [(state, sx.at[2:10, 16:80]), (conv_in, w1), (conv_out, w2), (background, bg)]
     ins += [(probe_in, probe)]
     loads = [pltpu.make_async_copy(a, b, load_sem.at[n]) for n, (a, b) in enumerate(ins)]
     for c in loads:
         c.start()
+    for a, b in OTHERS:
+        pl.semaphore_signal(barrier, inc=1, device_id=place(a, b)[1], device_id_type=MESH)
 
     def scatter(src, dst, sems):
-        def one(k, c):
-            t, to = place(k)
+        for a, b in OTHERS:
+            t, to = place(a, b)
             send(src.at[t], dst.at[me], (sems.at[0], sems.at[1]), to).start()
-            return c
-
-        lax.fori_loop(1, TILES, one, 0)
         own = pltpu.make_async_copy(src.at[me], dst.at[me], own_sem.at[0])
         own.start()
         own.wait()
 
-    def settle(src, dst, sem):
+    def settle(src, dst, sems, which):
         some = slice(0, TILES - 1)
-        pltpu.make_async_copy(src.at[some], dst.at[some], sem).wait()
+        pltpu.make_async_copy(src.at[some], dst.at[some], sems.at[which]).wait()
 
     def halo(field, which):
         copies = [
@@ -242,7 +245,7 @@
         for q in range(4)
     ]
 
-    settle(sbuf, r2, out_sem.at[1])
+    settle(sbuf, r2, out_sem, 1)
     cells, shares = [], []
     for t in range(TILES // 8):
         own = slice(8 * t, 8 * t + 8)
@@ -356,7 +359,7 @@
         y = gathered(prod, r * PITCH, COLS) + ax[2 + r, 16:80].astype(F32)
         grad[r] = y.astype(B16)
 
-    settle(qbuf, q2, back_sem.at[1])
+    settle(qbuf, q2, back_sem, 1)
     back = q2[:, 0, :].T[0:CAP]
     one = back.astype(B16)
     rest = back - one.astype(F32)
@@ -372,8 +375,8 @@
 
     for c in first + second + out4:
         c.wait_send()
-    settle(sbuf, r2, out_sem.at[0])
-    settle(qbuf, q2, back_sem.at[0])
+    settle(sbuf, r2, out_sem, 0)
+    settle(qbuf, q2, back_sem, 0)
 
 
 def on_device(
@@ -388,8 +391,8 @@
     grad, innov = pl.pallas_call(
         kernel,
         out_shape=(
-            jax.ShapeDtypeStruct((ROWS, COLS, CH), B16),
-            jax.ShapeDtypeStruct((1, COUNT), F32),
+            pltpu.VMEM((ROWS, COLS, CH), B16),
+            pltpu.VMEM((1, COUNT), F32),
         ),
         in_specs=[hbm] * 10,
         out_specs=(vmem, vmem),

time: 34.5 us -> 31.1 us (0.901)
  Pallas kernels: 30.7 us -> 29 us
  local copies, waits for them, and re-layouts: 2.96 us -> 1.3 us
    pallas_call x1, Pallas kernels: 30.7 us -> 29 us  [on_device(): pl.pallas_call(kernel, out_shape=(pltpu.VMEM((ROWS, COLS, CH), B16), pltp...]
    unnamed x2, local copies, waits for them, and re-layouts: 2.96 us -> 1.3 us
where the time goes in v3:
time: 31.1 us; the launch traced here: 31 us
  Pallas kernels  29 us (93%)
  local copies, waits for them, and re-layouts  1.3 us (4%)
  between operations  0.64 us (2%)
    pallas_call x1, Pallas kernels, on_device(): pl.pallas_call(kernel, out_shape=(pltpu.VMEM((ROWS, COLS, CH), B16), pltp...  29 us
    unnamed x2, local copies, waits for them, and re-layouts  1.3 us

profile of v3, /device:TPU:1, one launch (start us, length us, event | category | flops | bytes accessed | tf_op | source)
XLA Modules:
  0.0 31.0 jit_solution(11558013793031582624)
XLA Ops:
  0.6 29.0 %shard_map.113 = (bf16[8,64,256]{2,1,0:T(8,128)(2,1)S(1)}, f32[1,2048]{1,0:T(1,128)S(1)}) custom-call(s32[1,2048]{1,0:T(1,128)} %bitcast.6, s32[4,2048]{1,0:T(4,128)} %taps_in.1, f32[4,2048]{1,0:T(4,128)} %wts_in.1, f32[1,2048]{1,0:T(1,128)} %bitcast.7, f32[1,2048]{1,0:T(1,128)} %bitcast.8, f32[1,256]{1,0:T(1,128)} %bitcast.9, bf16[8,64,256]{2,1,0:T(8,128)(2,1)} %state.1, ...), custom_call_target="tpu_custom_call" | custom-call | tf_op jit(solution)/shard_map/pallas_call | solution.py:391
  29.7 0.7 %copy.14 = bf16[8,64,256]{2,1,0:T(8,128)(2,1)} copy(bf16[8,64,256]{2,1,0:T(8,128)(2,1)S(1)} %get-tuple-element.6) | data formatting | bytes 524288
  30.4 0.6 %copy.15 = f32[2048]{0:T(1024)} copy(f32[2048]{0:T(1024)S(1)} %bitcast.5) | data formatting | bytes 16384

commit v4 on v3

--- a/solution.py
+++ b/solution.py
@@ -30,6 +30,7 @@
 
 OTHERS = [(a, b) for a in range(LATS) for b in range(LONS) if (a, b) != (0, 0)]
 OTHERS.sort(key=lambda o: -hops(*o))
+LINES = [o for o in OTHERS if 0 in o]
 
 
 def iota(shape, dim):
@@ -99,7 +100,7 @@
     grad, innov,
     ids, taps, wts, vals, prec, probe, sx, mx, ax, bg, w1, w2, before, hx, mb, prod, dt, rank_s,
     packs, arrived, sbuf, r2, qbuf, q2, zs, zr,
-    load_sem, row_sem, pack_sem, out_sem, back_sem, z_sem, own_sem,
+    load_sem, row_sem, pack_sem, out_sem, back_sem, z_sem, own_sem, ready,
 ):
     la = lax.axis_index("lat")
     lo = lax.axis_index("lon")
@@ -126,8 +127,28 @@
     loads = [pltpu.make_async_copy(a, b, load_sem.at[n]) for n, (a, b) in enumerate(ins)]
     for c in loads:
         c.start()
-    for a, b in OTHERS:
+
+    def greet(a, b):
         pl.semaphore_signal(barrier, inc=1, device_id=place(a, b)[1], device_id_type=MESH)
+
+    def where(a, run, things):
+        def body():
+            for t in things:
+                run(t)
+
+        if a == 0:
+            body()
+        else:
+            pl.when(la > 0 if a < 0 else la < LATS - 1)(body)
+
+    for a in (-1, 1):
+        where(a, lambda b: greet(a, b), (-1, 1))
+    for a, b in LINES:
+        greet(a, b)
+
+    def each(copies, act):
+        for a in (-1, 1, 0):
+            where(a, act, [c for s, c in copies if s[0] == a])
 
     def scatter(src, dst, sems):
         for a, b in OTHERS:
@@ -143,18 +164,22 @@
 
     def halo(field, which):
         copies = [
-            send(field.at[2:4, 16:80], field.at[10:12, 16:80],
-                 (row_sem.at[which, 0, 0], row_sem.at[which, 0, 1]), near(-1, 0)),
-            send(field.at[8:10, 16:80], field.at[0:2, 16:80],
-                 (row_sem.at[which, 1, 0], row_sem.at[which, 1, 1]), near(1, 0)),
+            ((-1, 0), send(field.at[2:4, 16:80], field.at[10:12, 16:80],
+                           (row_sem.at[which, 0, 0], row_sem.at[which, 1, 1]), near(-1, 0))),
+            ((1, 0), send(field.at[8:10, 16:80], field.at[0:2, 16:80],
+                          (row_sem.at[which, 1, 0], row_sem.at[which, 0, 1]), near(1, 0))),
         ]
         for n, (a, b) in enumerate(CORNERS):
             m = CORNERS.index((-a, -b))
             copies.append(
-                send(packs.at[which, 0 if b < 0 else 1], arrived.at[which, m],
-                     (pack_sem.at[which, n, 0], pack_sem.at[which, m, 1]), near(a, b))
+                ((a, b), send(packs.at[which, 0 if b < 0 else 1], arrived.at[which, m],
+                              (pack_sem.at[which, n, 0], pack_sem.at[which, m, 1]), near(a, b)))
             )
         return copies
+
+    def arrive(copies):
+        back = {s: c for s, c in copies}
+        each([(s, back[-s[0], -s[1]]) for s in back], lambda c: c.wait_recv())
 
     def clear(field, low, high):
         @pl.when(la == 0)
@@ -199,15 +224,17 @@
 
     loads[5].wait()
     pack(sx, packs.at[0])
-    pl.semaphore_wait(barrier, TILES - 1)
+    ends = jnp.where((la == 0) | (la == LATS - 1), 2, 4)
+    pl.semaphore_wait(barrier, len(LINES) + ends)
+    for a in range(1, LATS):
+        pl.semaphore_signal(ready, inc=1, device_id=place(a, 0)[1], device_id_type=MESH)
     first = halo(sx, 0)
-    for c in first:
-        c.start()
+    each(first, lambda c: c.start())
+    pl.semaphore_wait(ready, LATS - 1)
     scatter(sbuf, r2, out_sem)
 
     loads[6].wait()
-    for c in first:
-        c.wait_recv()
+    arrive(first)
     unpack(sx, arrived.at[0])
     clear(sx, 2, 10)
     products(sx, 10, WIDE, w1, False, prod)
@@ -238,8 +265,7 @@
         mx[2 + r, 16:80] = d.astype(B16)
     pack(mx, packs.at[1])
     second = halo(mx, 1)
-    for c in second:
-        c.start()
+    each(second, lambda c: c.start())
     tables = [
         jnp.broadcast_to(jnp.concatenate(strips[2 * q : 2 * q + 2], axis=1), (8, 128))
         for q in range(4)
@@ -295,8 +321,8 @@
     out4 = []
     for n, (a, b) in enumerate(SIDES):
         m = SIDES.index((-a, -b))
-        out4.append(send(zs, zr.at[m], (z_sem.at[n, 0], z_sem.at[m, 1]), near(a, b)))
-        out4[-1].start()
+        out4.append(((a, b), send(zs, zr.at[m], (z_sem.at[n, 0], z_sem.at[m, 1]), near(a, b))))
+    each(out4, lambda c: c.start())
 
     scatter(qbuf, q2, back_sem)
 
@@ -324,11 +350,9 @@
     local = outer([(center, r, c) for r in range(ROWS) for c in range(4)])
     for r in range(ROWS):
         ax[2 + r, 16:80] = (mb[r] + local[r * 64 : (r + 1) * 64]).astype(B16)
-    for c in second:
-        c.wait_recv()
+    arrive(second)
     unpack(mx, arrived.at[1])
-    for c in out4:
-        c.wait_recv()
+    arrive(out4)
     around = {s: parted(zr[n]) for n, s in enumerate(SIDES)}
     for a, rows in ((-1, (6, 7)), (1, (0, 1))):
         piece = outer([(around[a, 0], r, c) for r in rows for c in range(4)])
@@ -373,8 +397,7 @@
         own = iota((CAP, 512), 0) == rank_s[0:1, cut].astype(I32)
         innov[0:1, cut] = jnp.sum(jnp.where(own, got, 0.0), axis=0, keepdims=True)
 
-    for c in first + second + out4:
-        c.wait_send()
+    each(first + second + out4, lambda c: c.wait_send())
     settle(sbuf, r2, out_sem, 0)
     settle(qbuf, q2, back_sem, 0)
 
@@ -428,6 +451,7 @@
             dma((2,)),
             dma((len(SIDES), 2)),
             dma((1,)),
+            pltpu.SemaphoreType.REGULAR,
         ],
         compiler_params=pltpu.CompilerParams(
             collective_id=0, has_side_effects=True, vmem_limit_bytes=56 * 2**20

time: 31.1 us -> 29.2 us (0.939)
  Pallas kernels: 29 us -> 27.1 us
    pallas_call x1, Pallas kernels: 29 us -> 27.1 us  [on_device(): pl.pallas_call(kernel, out_shape=(pltpu.VMEM((ROWS, COLS, CH), B16), pltp...]
where the time goes in v4:
time: 29.2 us; the launch traced here: 29.1 us
  Pallas kernels  27.1 us (93%)
  local copies, waits for them, and re-layouts  1.3 us (4%)
  between operations  0.64 us (2%)
    pallas_call x1, Pallas kernels, on_device(): pl.pallas_call(kernel, out_shape=(pltpu.VMEM((ROWS, COLS, CH), B16), pltp...  27.1 us
    unnamed x2, local copies, waits for them, and re-layouts  1.3 us

profile of v4, /device:TPU:1, one launch (start us, length us, event | category | flops | bytes accessed | tf_op | source)
XLA Modules:
  0.0 29.1 jit_solution(1889882864719196108)
XLA Ops:
  0.6 27.1 %shard_map.113 = (bf16[8,64,256]{2,1,0:T(8,128)(2,1)S(1)}, f32[1,2048]{1,0:T(1,128)S(1)}) custom-call(s32[1,2048]{1,0:T(1,128)} %bitcast.6, s32[4,2048]{1,0:T(4,128)} %taps_in.1, f32[4,2048]{1,0:T(4,128)} %wts_in.1, f32[1,2048]{1,0:T(1,128)} %bitcast.7, f32[1,2048]{1,0:T(1,128)} %bitcast.8, f32[1,256]{1,0:T(1,128)} %bitcast.9, bf16[8,64,256]{2,1,0:T(8,128)(2,1)} %state.1, ...), custom_call_target="tpu_custom_call" | custom-call | tf_op jit(solution)/shard_map/pallas_call | solution.py:414
  27.8 0.7 %copy.14 = bf16[8,64,256]{2,1,0:T(8,128)(2,1)} copy(bf16[8,64,256]{2,1,0:T(8,128)(2,1)S(1)} %get-tuple-element.6) | data formatting | bytes 524288
  28.5 0.6 %copy.15 = f32[2048]{0:T(1024)} copy(f32[2048]{0:T(1024)S(1)} %bitcast.5) | data formatting | bytes 16384

commit v5 on v4

--- a/solution.py
+++ b/solution.py
@@ -12,7 +12,6 @@
 F32 = jnp.float32
 I32 = jnp.int32
 ROWS, COLS, CH = 8, 64, 256
-WIDE = 96
 PITCH = 80
 LATS, LONS = 8, 16
 TILES = LATS * LONS
@@ -42,20 +41,59 @@
     return high, (x - high.astype(F32)).astype(B16)
 
 
-def products(field, rows, pitch, weights, flipped, prod):
-    count = rows * pitch
+def weighted(lhs, weights, flipped, j):
+    if flipped:
+        rhs = jnp.concatenate([weights[2 - i, 2 - j] for i in range(3)], axis=1)
+        return lax.dot_general(lhs, rhs, NT, preferred_element_type=F32)
+    rhs = jnp.concatenate([weights[i, j] for i in range(3)], axis=0)
+    return jnp.dot(lhs, rhs, preferred_element_type=F32)
+
+
+def windows(field, first, rows):
+    count = rows * field.shape[1]
+    return jnp.concatenate(
+        [field[first + i : first + i + rows].reshape(count, CH) for i in range(3)], axis=1
+    )
+
+
+def products(field, weights, flipped, prod):
+    lhs = windows(field, 0, ROWS)
+    for j in range(3):
+        out = weighted(lhs, weights, flipped, j)
+        prod[j, 0, 0 : ROWS * PITCH] = out[:, :128]
+        prod[j, 1, 0 : ROWS * PITCH] = out[:, 128:]
+
+
+def put(prod, j, row, out):
+    start = row * PITCH + 8
+    prod[j, 0, start : start + COLS] = out[:, :128]
+    prod[j, 1, start : start + COLS] = out[:, 128:]
+
+
+def inner(field, weights, flipped, prod, j):
+    out = weighted(windows(field, 2, 6), weights, flipped, j)
+    for n in range(6):
+        put(prod, j, 2 + n, out[n * COLS : (n + 1) * COLS])
+
+
+def border(field, edge, weights, flipped, prod):
+    sides = [
+        jnp.concatenate([edge[b, 2 * i : 2 * i + 24] for i in range(3)], axis=1) for b in range(2)
+    ]
     lhs = jnp.concatenate(
-        [field[i : i + rows].reshape(count, CH) for i in range(3)], axis=1
+        [windows(field, 0, 2), windows(field, 8, 2), jnp.concatenate(sides, axis=0).astype(B16)],
+        axis=0,
     )
     for j in range(3):
-        if flipped:
-            rhs = jnp.concatenate([weights[2 - i, 2 - j] for i in range(3)], axis=1)
-            out = lax.dot_general(lhs, rhs, NT, preferred_element_type=F32)
-        else:
-            rhs = jnp.concatenate([weights[i, j] for i in range(3)], axis=0)
-            out = jnp.dot(lhs, rhs, preferred_element_type=F32)
-        prod[j, 0, 0:count] = out[:, :128]
-        prod[j, 1, 0:count] = out[:, 128:]
+        out = weighted(lhs, weights, flipped, j)
+        for n, row in enumerate((0, 1, 8, 9)):
+            put(prod, j, row, out[n * COLS : (n + 1) * COLS])
+        for b in range(2):
+            for row in range(10):
+                at = 4 * COLS + 24 * b + 2 * row
+                start = row * PITCH + (72 if b else 6)
+                prod[j, 0, start : start + 2] = out[at : at + 2, :128]
+                prod[j, 1, start : start + 2] = out[at : at + 2, 128:]
 
 
 def gathered(prod, start, count):
@@ -74,31 +112,30 @@
     east = jnp.zeros((16, CH), F32)
     for r in range(ROWS):
         here = (sub == 2 * r) | (sub == 2 * r + 1)
-        x = field[2 + r, 16:32].astype(F32)
+        x = field[2 + r, 0:16].astype(F32)
         west = jnp.where(here, x if r == 0 else pltpu.roll(x, 2 * r, 0), west)
-        x = field[2 + r, 64:80].astype(F32)
+        x = field[2 + r, 48:64].astype(F32)
         east = jnp.where(here, x if r == 7 else pltpu.roll(x, (2 * r - 14) % 16, 0), east)
     packs[0] = west.astype(B16)
     packs[1] = east.astype(B16)
 
 
-def unpack(field, arrived):
+def assemble(edge, parts, north, south):
     for n, (a, b) in enumerate(CORNERS):
-        x = arrived[n].astype(F32)
-        for r in {-1: (6, 7), 0: range(8), 1: (0, 1)}[a]:
-            row = r + 2 + a * 8
-            shift = (14 - 2 * r) % 16 if b < 0 else (-2 * r) % 16
-            block = (x if shift == 0 else pltpu.roll(x, shift, 0)).astype(B16)
-            if b < 0:
-                field[row, 0:16] = block
-            else:
-                field[row, 80:96] = block
+        x = parts[n]
+        side = 0 if b < 0 else 1
+        if a < 0:
+            edge[side, 0:4] = jnp.where(north, x[12:16], 0.0)
+        elif a == 0:
+            edge[side, 4:20] = x
+        else:
+            edge[side, 20:24] = jnp.where(south, x[0:4], 0.0)
 
 
 def kernel(
     ids_in, taps_in, wts_in, vals_in, prec_in, probe_in, state, background, conv_in, conv_out,
     grad, innov,
-    ids, taps, wts, vals, prec, probe, sx, mx, ax, bg, w1, w2, before, hx, mb, prod, dt, rank_s,
+    ids, taps, wts, vals, prec, probe, edge, sx, mx, ax, bg, w1, w2, before, hx, mb, prod, dt, rank_s,
     packs, arrived, sbuf, r2, qbuf, q2, zs, zr,
     load_sem, row_sem, pack_sem, out_sem, back_sem, z_sem, own_sem, ready,
 ):
@@ -122,7 +159,7 @@
         return to[0] * LONS + to[1], to
 
     ins = [(ids_in, ids), (prec_in, prec), (taps_in, taps), (wts_in, wts), (vals_in, vals)]
-    ins += [(state, sx.at[2:10, 16:80]), (conv_in, w1), (conv_out, w2), (background, bg)]
+    ins += [(state, sx.at[2:10]), (conv_in, w1), (conv_out, w2), (background, bg)]
     ins += [(probe_in, probe)]
     loads = [pltpu.make_async_copy(a, b, load_sem.at[n]) for n, (a, b) in enumerate(ins)]
     for c in loads:
@@ -150,10 +187,12 @@
         for a in (-1, 1, 0):
             where(a, act, [c for s, c in copies if s[0] == a])
 
-    def scatter(src, dst, sems):
-        for a, b in OTHERS:
+    def depart(src, dst, sems, offsets):
+        for a, b in offsets:
             t, to = place(a, b)
             send(src.at[t], dst.at[me], (sems.at[0], sems.at[1]), to).start()
+
+    def stay(src, dst):
         own = pltpu.make_async_copy(src.at[me], dst.at[me], own_sem.at[0])
         own.start()
         own.wait()
@@ -164,9 +203,9 @@
 
     def halo(field, which):
         copies = [
-            ((-1, 0), send(field.at[2:4, 16:80], field.at[10:12, 16:80],
+            ((-1, 0), send(field.at[2:4], field.at[10:12],
                            (row_sem.at[which, 0, 0], row_sem.at[which, 1, 1]), near(-1, 0))),
-            ((1, 0), send(field.at[8:10, 16:80], field.at[0:2, 16:80],
+            ((1, 0), send(field.at[8:10], field.at[0:2],
                           (row_sem.at[which, 1, 0], row_sem.at[which, 0, 1]), near(1, 0))),
         ]
         for n, (a, b) in enumerate(CORNERS):
@@ -231,22 +270,25 @@
     first = halo(sx, 0)
     each(first, lambda c: c.start())
     pl.semaphore_wait(ready, LATS - 1)
-    scatter(sbuf, r2, out_sem)
+    depart(sbuf, r2, out_sem, OTHERS)
+    stay(sbuf, r2)
 
     loads[6].wait()
+    for j in range(3):
+        inner(sx, w1, False, prod, j)
     arrive(first)
-    unpack(sx, arrived.at[0])
+    assemble(edge, [arrived[0, n].astype(F32) for n in range(6)], la > 0, la < LATS - 1)
     clear(sx, 2, 10)
-    products(sx, 10, WIDE, w1, False, prod)
+    border(sx, edge, w1, False, prod)
     for r in range(10):
-        b = gathered(prod, r * WIDE + 14, PITCH)
+        b = gathered(prod, r * PITCH + 6, PITCH)
         before[r] = b
         hx[r] = (b / (1.0 + jnp.exp(-b))).astype(B16)
     clear(hx, 1, 9)
 
     for c in loads[7:]:
         c.wait()
-    products(hx, 8, PITCH, w2, False, prod)
+    products(hx, w2, False, prod)
     pr = probe[...]
     ph, plow = halves(pr)
     sub16 = iota((16, CH), 0)
@@ -255,14 +297,14 @@
     ).astype(B16)
     strips = []
     for r in range(ROWS):
-        m = gathered(prod, r * PITCH, COLS) + sx[2 + r, 16:80].astype(F32)
+        m = gathered(prod, r * PITCH, COLS) + sx[2 + r].astype(F32)
         high, low = halves(m)
         s = lax.dot_general(readout, high, NT, preferred_element_type=F32)
         t = lax.dot_general(readout, low, NT, preferred_element_type=F32)
         strips.append(s[0:1] + s[1:2] + t[0:1])
         d = m - bg[r].astype(F32)
         mb[r] = d
-        mx[2 + r, 16:80] = d.astype(B16)
+        mx[2 + r] = d.astype(B16)
     pack(mx, packs.at[1])
     second = halo(mx, 1)
     each(second, lambda c: c.start())
@@ -324,11 +366,11 @@
         out4.append(((a, b), send(zs, zr.at[m], (z_sem.at[n, 0], z_sem.at[m, 1]), near(a, b))))
     each(out4, lambda c: c.start())
 
-    scatter(qbuf, q2, back_sem)
-
+    stay(qbuf, q2)
     group = iota((16, 128), 1) // 32
     base = jnp.where(iota((128, CH), 0) // 64 == 0, ph.astype(F32), plow.astype(F32)).astype(B16)
     sub = iota((16, 128), 0)
+    odd = lax.bitwise_and(sub, 1)
     spot = lax.bitwise_and(iota((16, 128), 1), 31)
     marks = [spot == sub, spot == sub + 16]
 
@@ -347,40 +389,50 @@
         return jnp.dot(lhs, base, preferred_element_type=F32)
 
     center = parted(fold)
-    local = outer([(center, r, c) for r in range(ROWS) for c in range(4)])
     for r in range(ROWS):
-        ax[2 + r, 16:80] = (mb[r] + local[r * 64 : (r + 1) * 64]).astype(B16)
+        local = outer([(center, r, c) for c in range(4)])
+        ax[2 + r] = (mb[r] + local).astype(B16)
+        depart(qbuf, q2, back_sem, OTHERS[r * 10 : r * 10 + 10])
+    for j in range(3):
+        inner(ax, w2, True, prod, j)
+        depart(qbuf, q2, back_sem, OTHERS[80 + 16 * j : 96 + 16 * j])
+
     arrive(second)
-    unpack(mx, arrived.at[1])
     arrive(out4)
     around = {s: parted(zr[n]) for n, s in enumerate(SIDES)}
     for a, rows in ((-1, (6, 7)), (1, (0, 1))):
         piece = outer([(around[a, 0], r, c) for r in rows for c in range(4)])
         for n, r in enumerate(rows):
             row = r + 2 + a * 8
-            ax[row, 16:80] = (
-                mx[row, 16:80].astype(F32) + piece[n * 64 : (n + 1) * 64]
-            ).astype(B16)
-    for b, c, at in ((-1, 3, 0), (1, 0, 80)):
-        spots = [(a, r) for a, rows in ((-1, (6, 7)), (0, range(8)), (1, (0, 1))) for r in rows]
-        piece = outer([(around[a, b], r, c) for a, r in spots])
-        for n, (a, r) in enumerate(spots):
-            row = r + 2 + a * 8
-            ax[row, at : at + 16] = (
-                mx[row, at : at + 16].astype(F32) + piece[n * 16 : (n + 1) * 16]
-            ).astype(B16)
+            ax[row] = (mx[row].astype(F32) + piece[n * 64 : (n + 1) * 64]).astype(B16)
+    strips = []
+    for a, b in CORNERS:
+        z = around[a, b]
+        if b < 0:
+            z = jnp.where(odd == 1, z, pltpu.roll(z, 15, 0))
+            hit = spot == odd + 30
+        else:
+            z = jnp.where(odd == 0, z, pltpu.roll(z, 1, 0))
+            hit = spot == odd
+        strips.append(jnp.where(hit, z, 0.0).astype(B16))
+    piece = jnp.dot(jnp.concatenate(strips, axis=0), base, preferred_element_type=F32)
+    parts = [
+        (arrived[1, n].astype(F32) + piece[16 * n : 16 * n + 16]).astype(B16).astype(F32)
+        for n in range(6)
+    ]
+    assemble(edge, parts, la > 0, la < LATS - 1)
     clear(ax, 2, 10)
 
-    products(ax, 10, WIDE, w2, True, prod)
+    border(ax, edge, w2, True, prod)
     for r in range(10):
         x = before[r]
         sigma = 1.0 / (1.0 + jnp.exp(-x))
-        y = gathered(prod, r * WIDE + 14, PITCH) * sigma * (1.0 + x * (1.0 - sigma))
+        y = gathered(prod, r * PITCH + 6, PITCH) * sigma * (1.0 + x * (1.0 - sigma))
         hx[r] = y.astype(B16)
     clear(hx, 1, 9)
-    products(hx, 8, PITCH, w1, True, prod)
+    products(hx, w1, True, prod)
     for r in range(ROWS):
-        y = gathered(prod, r * PITCH, COLS) + ax[2 + r, 16:80].astype(F32)
+        y = gathered(prod, r * PITCH, COLS) + ax[2 + r].astype(F32)
         grad[r] = y.astype(B16)
 
     settle(qbuf, q2, back_sem, 1)
@@ -409,7 +461,7 @@
     vmem = pl.BlockSpec(memory_space=pltpu.VMEM)
     hbm = pl.BlockSpec(memory_space=pl.ANY)
     dma = pltpu.SemaphoreType.DMA
-    wide = pltpu.VMEM((12, WIDE, CH), B16)
+    wide = pltpu.VMEM((12, COLS, CH), B16)
     kshape = (3, 3, CH, CH)
     grad, innov = pl.pallas_call(
         kernel,
@@ -426,6 +478,7 @@
             pltpu.VMEM((1, COUNT), F32),
             pltpu.VMEM((1, COUNT), F32),
             pltpu.VMEM((1, CH), F32),
+            pltpu.VMEM((2, 32, CH), F32),
             wide, wide, wide,
             pltpu.VMEM((ROWS, COLS, CH), B16),
             pltpu.VMEM(kshape, B16),
@@ -433,7 +486,7 @@
             pltpu.VMEM((10, PITCH, CH), F32),
             pltpu.VMEM((10, PITCH, CH), B16),
             pltpu.VMEM((ROWS, COLS, CH), F32),
-            pltpu.VMEM((3, 2, 10 * WIDE + 64, 128), F32),
+            pltpu.VMEM((3, 2, 10 * PITCH + 64, 128), F32),
             pltpu.VMEM((TILES, COUNT), B16),
             pltpu.VMEM((1, COUNT), F32),
             pltpu.VMEM((2, 2, 16, CH), B16),

time: 29.2 us -> 28.7 us (0.983)
  Pallas kernels: 27.1 us -> 26.6 us
    pallas_call x1, Pallas kernels: 27.1 us -> 26.6 us  [on_device(): pl.pallas_call(kernel, out_shape=(pltpu.VMEM((ROWS, COLS, CH), B16), pltp...]
where the time goes in v5:
time: 28.7 us; the launch traced here: 28.6 us
  Pallas kernels  26.6 us (93%)
  local copies, waits for them, and re-layouts  1.3 us (5%)
  between operations  0.64 us (2%)
    pallas_call x1, Pallas kernels, on_device(): pl.pallas_call(kernel, out_shape=(pltpu.VMEM((ROWS, COLS, CH), B16), pltp...  26.6 us
    unnamed x2, local copies, waits for them, and re-layouts  1.3 us

profile of v5, /device:TPU:1, one launch (start us, length us, event | category | flops | bytes accessed | tf_op | source)
XLA Modules:
  0.0 28.6 jit_solution(4806320259764334344)
XLA Ops:
  0.6 26.6 %shard_map.113 = (bf16[8,64,256]{2,1,0:T(8,128)(2,1)S(1)}, f32[1,2048]{1,0:T(1,128)S(1)}) custom-call(s32[1,2048]{1,0:T(1,128)} %bitcast.6, s32[4,2048]{1,0:T(4,128)} %taps_in.1, f32[4,2048]{1,0:T(4,128)} %wts_in.1, f32[1,2048]{1,0:T(1,128)} %bitcast.7, f32[1,2048]{1,0:T(1,128)} %bitcast.8, f32[1,256]{1,0:T(1,128)} %bitcast.9, bf16[8,64,256]{2,1,0:T(8,128)(2,1)} %state.1, ...), custom_call_target="tpu_custom_call" | custom-call | tf_op jit(solution)/shard_map/pallas_call | solution.py:466
  27.3 0.7 %copy.14 = bf16[8,64,256]{2,1,0:T(8,128)(2,1)} copy(bf16[8,64,256]{2,1,0:T(8,128)(2,1)S(1)} %get-tuple-element.6) | data formatting | bytes 524288
  28.0 0.6 %copy.15 = f32[2048]{0:T(1024)} copy(f32[2048]{0:T(1024)S(1)} %bitcast.5) | data formatting | bytes 16384

commit v6 on v5

--- a/solution.py
+++ b/solution.py
@@ -29,6 +29,8 @@
 
 OTHERS = [(a, b) for a in range(LATS) for b in range(LONS) if (a, b) != (0, 0)]
 OTHERS.sort(key=lambda o: -hops(*o))
+FIRST = 0
+ROUND = sorted(range(1, LONS), key=lambda b: -hops(0, b))
 LINES = [o for o in OTHERS if 0 in o]
 
 
@@ -135,7 +137,7 @@
 def kernel(
     ids_in, taps_in, wts_in, vals_in, prec_in, probe_in, state, background, conv_in, conv_out,
     grad, innov,
-    ids, taps, wts, vals, prec, probe, edge, sx, mx, ax, bg, w1, w2, before, hx, mb, prod, dt, rank_s,
+    ids, taps, wts, vals, prec, probe, edge, sx, mx, ax, bg, w1, w2, slope, hx, mb, prod, dt, rank_s,
     packs, arrived, sbuf, r2, qbuf, q2, zs, zr,
     load_sem, row_sem, pack_sem, out_sem, back_sem, z_sem, own_sem, ready,
 ):
@@ -162,7 +164,7 @@
     ins += [(state, sx.at[2:10]), (conv_in, w1), (conv_out, w2), (background, bg)]
     ins += [(probe_in, probe)]
     loads = [pltpu.make_async_copy(a, b, load_sem.at[n]) for n, (a, b) in enumerate(ins)]
-    for c in loads:
+    for c in loads[:5]:
         c.start()
 
     def greet(a, b):
@@ -182,20 +184,26 @@
         where(a, lambda b: greet(a, b), (-1, 1))
     for a, b in LINES:
         greet(a, b)
+    for c in loads[5:]:
+        c.start()
 
     def each(copies, act):
         for a in (-1, 1, 0):
             where(a, act, [c for s, c in copies if s[0] == a])
+
+    def give(src, dst, sems, row, b):
+        to = (row, lax.bitwise_and(lo + b, LONS - 1))
+        send(src.at[row * LONS + to[1]], dst.at[me], (sems.at[0], sems.at[1]), to).start()
 
     def depart(src, dst, sems, offsets):
         for a, b in offsets:
             t, to = place(a, b)
             send(src.at[t], dst.at[me], (sems.at[0], sems.at[1]), to).start()
 
-    def stay(src, dst):
-        own = pltpu.make_async_copy(src.at[me], dst.at[me], own_sem.at[0])
+    def stay(src, dst, n):
+        own = pltpu.make_async_copy(src.at[me], dst.at[me], own_sem.at[n])
         own.start()
-        own.wait()
+        return own
 
     def settle(src, dst, sems, which):
         some = slice(0, TILES - 1)
@@ -266,24 +274,34 @@
     ends = jnp.where((la == 0) | (la == LATS - 1), 2, 4)
     pl.semaphore_wait(barrier, len(LINES) + ends)
     for a in range(1, LATS):
-        pl.semaphore_signal(ready, inc=1, device_id=place(a, 0)[1], device_id_type=MESH)
+        pl.semaphore_signal(
+            ready.at[la], inc=1, device_id=place(a, 0)[1], device_id_type=MESH
+        )
     first = halo(sx, 0)
     each(first, lambda c: c.start())
-    pl.semaphore_wait(ready, LATS - 1)
-    depart(sbuf, r2, out_sem, OTHERS)
-    stay(sbuf, r2)
-
     loads[6].wait()
     for j in range(3):
         inner(sx, w1, False, prod, j)
+    for row in range(LATS):
+
+        @pl.when(la != row)
+        def _(row=row):
+            pl.semaphore_wait(ready.at[row], 1)
+            give(sbuf, r2, out_sem, row, 0)
+
+        for b in ROUND:
+            give(sbuf, r2, out_sem, row, b)
+    kept = stay(sbuf, r2, 0)
+
     arrive(first)
     assemble(edge, [arrived[0, n].astype(F32) for n in range(6)], la > 0, la < LATS - 1)
     clear(sx, 2, 10)
     border(sx, edge, w1, False, prod)
     for r in range(10):
         b = gathered(prod, r * PITCH + 6, PITCH)
-        before[r] = b
-        hx[r] = (b / (1.0 + jnp.exp(-b))).astype(B16)
+        sigma = 1.0 / (1.0 + jnp.exp(-b))
+        slope[r] = sigma * (1.0 + b * (1.0 - sigma))
+        hx[r] = (b * sigma).astype(B16)
     clear(hx, 1, 9)
 
     for c in loads[7:]:
@@ -313,6 +331,7 @@
         for q in range(4)
     ]
 
+    kept.wait()
     settle(sbuf, r2, out_sem, 1)
     cells, shares = [], []
     for t in range(TILES // 8):
@@ -332,6 +351,7 @@
         cells.append(cell)
         shares.append(w * res)
 
+    depart(qbuf, q2, back_sem, OTHERS[:FIRST])
     total = jnp.zeros((256, 256), F32)
     for t in range(0, TILES // 8, 2):
         cell = jnp.concatenate(cells[t : t + 2], axis=1)
@@ -366,7 +386,8 @@
         out4.append(((a, b), send(zs, zr.at[m], (z_sem.at[n, 0], z_sem.at[m, 1]), near(a, b))))
     each(out4, lambda c: c.start())
 
-    stay(qbuf, q2)
+    depart(qbuf, q2, back_sem, OTHERS[FIRST:])
+    kept = stay(qbuf, q2, 1)
     group = iota((16, 128), 1) // 32
     base = jnp.where(iota((128, CH), 0) // 64 == 0, ph.astype(F32), plow.astype(F32)).astype(B16)
     sub = iota((16, 128), 0)
@@ -392,10 +413,8 @@
     for r in range(ROWS):
         local = outer([(center, r, c) for c in range(4)])
         ax[2 + r] = (mb[r] + local).astype(B16)
-        depart(qbuf, q2, back_sem, OTHERS[r * 10 : r * 10 + 10])
     for j in range(3):
         inner(ax, w2, True, prod, j)
-        depart(qbuf, q2, back_sem, OTHERS[80 + 16 * j : 96 + 16 * j])
 
     arrive(second)
     arrive(out4)
@@ -425,16 +444,14 @@
 
     border(ax, edge, w2, True, prod)
     for r in range(10):
-        x = before[r]
-        sigma = 1.0 / (1.0 + jnp.exp(-x))
-        y = gathered(prod, r * PITCH + 6, PITCH) * sigma * (1.0 + x * (1.0 - sigma))
-        hx[r] = y.astype(B16)
+        hx[r] = (gathered(prod, r * PITCH + 6, PITCH) * slope[r]).astype(B16)
     clear(hx, 1, 9)
     products(hx, w1, True, prod)
     for r in range(ROWS):
         y = gathered(prod, r * PITCH, COLS) + ax[2 + r].astype(F32)
         grad[r] = y.astype(B16)
 
+    kept.wait()
     settle(qbuf, q2, back_sem, 1)
     back = q2[:, 0, :].T[0:CAP]
     one = back.astype(B16)
@@ -503,8 +520,8 @@
             dma((2,)),
             dma((2,)),
             dma((len(SIDES), 2)),
-            dma((1,)),
-            pltpu.SemaphoreType.REGULAR,
+            dma((2,)),
+            pltpu.SemaphoreType.REGULAR((LATS,)),
         ],
         compiler_params=pltpu.CompilerParams(
             collective_id=0, has_side_effects=True, vmem_limit_bytes=56 * 2**20

time: 28.7 us -> 27.7 us (0.965)
  Pallas kernels: 26.6 us -> 25.7 us
    pallas_call x1, Pallas kernels: 26.6 us -> 25.7 us  [on_device(): pl.pallas_call(kernel, out_shape=(pltpu.VMEM((ROWS, COLS, CH), B16), pltp...]
where the time goes in v6:
time: 27.7 us; the launch traced here: 27.6 us
  Pallas kernels  25.7 us (93%)
  local copies, waits for them, and re-layouts  1.3 us (5%)
  between operations  0.64 us (2%)
    pallas_call x1, Pallas kernels, on_device(): pl.pallas_call(kernel, out_shape=(pltpu.VMEM((ROWS, COLS, CH), B16), pltp...  25.7 us
    unnamed x2, local copies, waits for them, and re-layouts  1.3 us

profile of v6, /device:TPU:1, one launch (start us, length us, event | category | flops | bytes accessed | tf_op | source)
XLA Modules:
  0.0 27.6 jit_solution(10746921781686924315)
XLA Ops:
  0.6 25.7 %shard_map.113 = (bf16[8,64,256]{2,1,0:T(8,128)(2,1)S(1)}, f32[1,2048]{1,0:T(1,128)S(1)}) custom-call(s32[1,2048]{1,0:T(1,128)} %bitcast.6, s32[4,2048]{1,0:T(4,128)} %taps_in.1, f32[4,2048]{1,0:T(4,128)} %wts_in.1, f32[1,2048]{1,0:T(1,128)} %bitcast.7, f32[1,2048]{1,0:T(1,128)} %bitcast.8, f32[1,256]{1,0:T(1,128)} %bitcast.9, bf16[8,64,256]{2,1,0:T(8,128)(2,1)} %state.1, ...), custom_call_target="tpu_custom_call" | custom-call | tf_op jit(solution)/shard_map/pallas_call | solution.py:483
  26.3 0.7 %copy.14 = bf16[8,64,256]{2,1,0:T(8,128)(2,1)} copy(bf16[8,64,256]{2,1,0:T(8,128)(2,1)S(1)} %get-tuple-element.6) | data formatting | bytes 524288
  27.0 0.6 %copy.15 = f32[2048]{0:T(1024)} copy(f32[2048]{0:T(1024)S(1)} %bitcast.5) | data formatting | bytes 16384

commit v7 on v6

--- a/solution.py
+++ b/solution.py
@@ -58,12 +58,24 @@
     )
 
 
-def products(field, weights, flipped, prod):
-    lhs = windows(field, 0, ROWS)
+def products(field, sides, weights, flipped, prod):
+    ends = [jnp.concatenate([sides[b, i : i + ROWS] for i in range(3)], axis=1) for b in range(2)]
+    lhs = jnp.concatenate(
+        [windows(field, 0, ROWS), jnp.concatenate(ends, axis=0).astype(B16)], axis=0
+    )
     for j in range(3):
         out = weighted(lhs, weights, flipped, j)
-        prod[j, 0, 0 : ROWS * PITCH] = out[:, :128]
-        prod[j, 1, 0 : ROWS * PITCH] = out[:, 128:]
+        for row in range(ROWS):
+            put(prod, j, row, out[row * COLS : (row + 1) * COLS])
+        at = ROWS * COLS
+        place_column(prod, j, 7, out[at : at + ROWS])
+        place_column(prod, j, 72, out[at + ROWS : at + 2 * ROWS])
+
+
+def place_column(prod, j, start, out):
+    rows = pl.ds(start, out.shape[0], stride=PITCH)
+    prod[j, 0, rows, :] = out[:, :128]
+    prod[j, 1, rows, :] = out[:, 128:]
 
 
 def put(prod, j, row, out):
@@ -80,7 +92,12 @@
 
 def border(field, edge, weights, flipped, prod):
     sides = [
-        jnp.concatenate([edge[b, 2 * i : 2 * i + 24] for i in range(3)], axis=1) for b in range(2)
+        jnp.concatenate(
+            [edge[b, h, pl.ds(2 * i + c, 16, stride=2), :] for i in range(3) for h in range(2)],
+            axis=1,
+        )
+        for b in range(2)
+        for c in range(2)
     ]
     lhs = jnp.concatenate(
         [windows(field, 0, 2), windows(field, 8, 2), jnp.concatenate(sides, axis=0).astype(B16)],
@@ -90,12 +107,24 @@
         out = weighted(lhs, weights, flipped, j)
         for n, row in enumerate((0, 1, 8, 9)):
             put(prod, j, row, out[n * COLS : (n + 1) * COLS])
-        for b in range(2):
-            for row in range(10):
-                at = 4 * COLS + 24 * b + 2 * row
-                start = row * PITCH + (72 if b else 6)
-                prod[j, 0, start : start + 2] = out[at : at + 2, :128]
-                prod[j, 1, start : start + 2] = out[at : at + 2, 128:]
+        for n, start in enumerate((6, 7, 72, 73)):
+            at = 4 * COLS + 16 * n
+            place_column(prod, j, start, out[at : at + 10])
+
+
+def columns(prod, start):
+    parts = [
+        prod[0, h, pl.ds(start, 10, stride=PITCH), :]
+        + prod[1, h, pl.ds(start + 1, 10, stride=PITCH), :]
+        + prod[2, h, pl.ds(start + 2, 10, stride=PITCH), :]
+        for h in range(2)
+    ]
+    return jnp.concatenate(parts, axis=1)
+
+
+def silu_parts(x):
+    sigma = 1.0 / (1.0 + jnp.exp(-x))
+    return x * sigma, sigma * (1.0 + x * (1.0 - sigma))
 
 
 def gathered(prod, start, count):
@@ -126,18 +155,20 @@
     for n, (a, b) in enumerate(CORNERS):
         x = parts[n]
         side = 0 if b < 0 else 1
-        if a < 0:
-            edge[side, 0:4] = jnp.where(north, x[12:16], 0.0)
-        elif a == 0:
-            edge[side, 4:20] = x
-        else:
-            edge[side, 20:24] = jnp.where(south, x[0:4], 0.0)
+        for h in range(2):
+            y = x[:, h * 128 : (h + 1) * 128]
+            if a < 0:
+                edge[side, h, 0:4] = jnp.where(north, y[12:16], 0.0)
+            elif a == 0:
+                edge[side, h, 4:20] = y
+            else:
+                edge[side, h, 20:24] = jnp.where(south, y[0:4], 0.0)
 
 
 def kernel(
     ids_in, taps_in, wts_in, vals_in, prec_in, probe_in, state, background, conv_in, conv_out,
     grad, innov,
-    ids, taps, wts, vals, prec, probe, edge, sx, mx, ax, bg, w1, w2, slope, hx, mb, prod, dt, rank_s,
+    ids, taps, wts, vals, prec, probe, edge, sx, mx, ax, bg, w1, w2, slope, slope_side, hx, side, mb, prod, dt, rank_s,
     packs, arrived, sbuf, r2, qbuf, q2, zs, zr,
     load_sem, row_sem, pack_sem, out_sem, back_sem, z_sem, own_sem, ready,
 ):
@@ -298,38 +329,40 @@
     clear(sx, 2, 10)
     border(sx, edge, w1, False, prod)
     for r in range(10):
-        b = gathered(prod, r * PITCH + 6, PITCH)
-        sigma = 1.0 / (1.0 + jnp.exp(-b))
-        slope[r] = sigma * (1.0 + b * (1.0 - sigma))
-        hx[r] = (b * sigma).astype(B16)
+        y, slope[r] = silu_parts(gathered(prod, r * PITCH + 7, COLS))
+        hx[r] = y.astype(B16)
+    row10 = iota((10, CH), 0)
+    outside = ((row10 == 0) & (la == 0)) | ((row10 == 9) & (la == LATS - 1))
+    for b in range(2):
+        y, slope_side[b, 0:10] = silu_parts(columns(prod, 71 * b + 6 * (1 - b)))
+        side[b, 0:10] = jnp.where(outside, 0.0, y)
     clear(hx, 1, 9)
 
     for c in loads[7:]:
         c.wait()
-    products(hx, w2, False, prod)
+    products(hx, side, w2, False, prod)
     pr = probe[...]
     ph, plow = halves(pr)
     sub16 = iota((16, CH), 0)
     readout = jnp.where(
         sub16 == 0, ph.astype(F32), jnp.where(sub16 == 1, plow.astype(F32), 0.0)
     ).astype(B16)
-    strips = []
+    highs, lows = [], []
     for r in range(ROWS):
-        m = gathered(prod, r * PITCH, COLS) + sx[2 + r].astype(F32)
+        m = gathered(prod, r * PITCH + 7, COLS) + sx[2 + r].astype(F32)
         high, low = halves(m)
-        s = lax.dot_general(readout, high, NT, preferred_element_type=F32)
-        t = lax.dot_general(readout, low, NT, preferred_element_type=F32)
-        strips.append(s[0:1] + s[1:2] + t[0:1])
+        highs.append(high)
+        lows.append(low)
         d = m - bg[r].astype(F32)
         mb[r] = d
         mx[2 + r] = d.astype(B16)
     pack(mx, packs.at[1])
     second = halo(mx, 1)
     each(second, lambda c: c.start())
-    tables = [
-        jnp.broadcast_to(jnp.concatenate(strips[2 * q : 2 * q + 2], axis=1), (8, 128))
-        for q in range(4)
-    ]
+    s = lax.dot_general(readout, jnp.concatenate(highs, axis=0), NT, preferred_element_type=F32)
+    t = lax.dot_general(readout, jnp.concatenate(lows, axis=0), NT, preferred_element_type=F32)
+    scalar = s[0:1] + s[1:2] + t[0:1]
+    tables = [jnp.broadcast_to(scalar[:, q * 128 : (q + 1) * 128], (8, 128)) for q in range(4)]
 
     kept.wait()
     settle(sbuf, r2, out_sem, 1)
@@ -352,26 +385,22 @@
         shares.append(w * res)
 
     depart(qbuf, q2, back_sem, OTHERS[:FIRST])
-    total = jnp.zeros((256, 256), F32)
+    total = jnp.zeros((128, 256), F32)
     for t in range(0, TILES // 8, 2):
         cell = jnp.concatenate(cells[t : t + 2], axis=1)
         share = jnp.concatenate(shares[t : t + 2], axis=1)
         upper_cell = lax.shift_right_logical(cell, 5)
         lower_cell = lax.bitwise_and(cell, 31)
-        top = share.astype(B16).astype(F32)
-        low = share - top
-        tops, lows, marks = [], [], []
+        tops, marks = [], []
         for g in range(8):
             hit = iota((16, 256), 0) == upper_cell[g : g + 1]
-            tops.append(jnp.where(hit, top[g : g + 1], 0.0).astype(B16))
-            lows.append(jnp.where(hit, low[g : g + 1], 0.0).astype(B16))
+            tops.append(jnp.where(hit, share[g : g + 1], 0.0).astype(B16))
             marks.append(
                 jnp.where(iota((32, 256), 0) == lower_cell[g : g + 1], 1.0, 0.0).astype(B16)
             )
-        lhs = jnp.concatenate(tops + lows, axis=0)
+        lhs = jnp.concatenate(tops, axis=0)
         rhs = jnp.concatenate(marks, axis=0)
         total = total + lax.dot_general(lhs, rhs, NT, preferred_element_type=F32)
-    total = total[0:128] + total[128:256]
     total = jnp.where(iota((128, 256), 0) // 16 == iota((128, 256), 1) // 32, total, 0.0)
     fold = total[0:16]
     for g in range(1, 8):
@@ -444,11 +473,14 @@
 
     border(ax, edge, w2, True, prod)
     for r in range(10):
-        hx[r] = (gathered(prod, r * PITCH + 6, PITCH) * slope[r]).astype(B16)
+        hx[r] = (gathered(prod, r * PITCH + 7, COLS) * slope[r]).astype(B16)
+    for b in range(2):
+        y = columns(prod, 71 * b + 6 * (1 - b)) * slope_side[b, 0:10]
+        side[b, 0:10] = jnp.where(outside, 0.0, y)
     clear(hx, 1, 9)
-    products(hx, w1, True, prod)
+    products(hx, side, w1, True, prod)
     for r in range(ROWS):
-        y = gathered(prod, r * PITCH, COLS) + ax[2 + r].astype(F32)
+        y = gathered(prod, r * PITCH + 7, COLS) + ax[2 + r].astype(F32)
         grad[r] = y.astype(B16)
 
     kept.wait()
@@ -495,13 +527,15 @@
             pltpu.VMEM((1, COUNT), F32),
             pltpu.VMEM((1, COUNT), F32),
             pltpu.VMEM((1, CH), F32),
-            pltpu.VMEM((2, 32, CH), F32),
+            pltpu.VMEM((2, 2, 40, 128), F32),
             wide, wide, wide,
             pltpu.VMEM((ROWS, COLS, CH), B16),
             pltpu.VMEM(kshape, B16),
             pltpu.VMEM(kshape, B16),
-            pltpu.VMEM((10, PITCH, CH), F32),
-            pltpu.VMEM((10, PITCH, CH), B16),
+            pltpu.VMEM((10, COLS, CH), F32),
+            pltpu.VMEM((2, 16, CH), F32),
+            pltpu.VMEM((10, COLS, CH), B16),
+            pltpu.VMEM((2, 16, CH), F32),
             pltpu.VMEM((ROWS, COLS, CH), F32),
             pltpu.VMEM((3, 2, 10 * PITCH + 64, 128), F32),
             pltpu.VMEM((TILES, COUNT), B16),

time: 27.7 us -> 27.4 us (0.989)
  Pallas kernels: 25.7 us -> 25.3 us
    pallas_call x1, Pallas kernels: 25.7 us -> 25.3 us  [on_device(): pl.pallas_call(kernel, out_shape=(pltpu.VMEM((ROWS, COLS, CH), B16), pltp...]
where the time goes in v7:
time: 27.4 us; the launch traced here: 27.3 us
  Pallas kernels  25.3 us (92%)
  local copies, waits for them, and re-layouts  1.3 us (5%)
  between operations  0.64 us (2%)
    pallas_call x1, Pallas kernels, on_device(): pl.pallas_call(kernel, out_shape=(pltpu.VMEM((ROWS, COLS, CH), B16), pltp...  25.3 us
    unnamed x2, local copies, waits for them, and re-layouts  1.3 us

profile of v7, /device:TPU:1, one launch (start us, length us, event | category | flops | bytes accessed | tf_op | source)
XLA Modules:
  0.0 27.3 jit_solution(5738849551285447458)
XLA Ops:
  0.6 25.3 %shard_map.113 = (bf16[8,64,256]{2,1,0:T(8,128)(2,1)S(1)}, f32[1,2048]{1,0:T(1,128)S(1)}) custom-call(s32[1,2048]{1,0:T(1,128)} %bitcast.6, s32[4,2048]{1,0:T(4,128)} %taps_in.1, f32[4,2048]{1,0:T(4,128)} %wts_in.1, f32[1,2048]{1,0:T(1,128)} %bitcast.7, f32[1,2048]{1,0:T(1,128)} %bitcast.8, f32[1,256]{1,0:T(1,128)} %bitcast.9, bf16[8,64,256]{2,1,0:T(8,128)(2,1)} %state.1, ...), custom_call_target="tpu_custom_call" | custom-call | tf_op jit(solution)/shard_map/pallas_call | solution.py:515
  26.0 0.7 %copy.14 = bf16[8,64,256]{2,1,0:T(8,128)(2,1)} copy(bf16[8,64,256]{2,1,0:T(8,128)(2,1)S(1)} %get-tuple-element.6) | data formatting | bytes 524288
  26.7 0.6 %copy.15 = f32[2048]{0:T(1024)} copy(f32[2048]{0:T(1024)S(1)} %bitcast.5) | data formatting | bytes 16384

commit v8 on v7

--- a/solution.py
+++ b/solution.py
@@ -29,7 +29,6 @@
 
 OTHERS = [(a, b) for a in range(LATS) for b in range(LONS) if (a, b) != (0, 0)]
 OTHERS.sort(key=lambda o: -hops(*o))
-FIRST = 0
 ROUND = sorted(range(1, LONS), key=lambda b: -hops(0, b))
 LINES = [o for o in OTHERS if 0 in o]
 
@@ -259,14 +258,11 @@
         back = {s: c for s, c in copies}
         each([(s, back[-s[0], -s[1]]) for s in back], lambda c: c.wait_recv())
 
-    def clear(field, low, high):
-        @pl.when(la == 0)
-        def _():
-            field[0:low] = jnp.zeros((low,) + field.shape[1:], field.dtype)
-
-        @pl.when(la == LATS - 1)
-        def _():
-            field[high:] = jnp.zeros((field.shape[0] - high,) + field.shape[1:], field.dtype)
+    inside = {-1: la > 0, 0: True, 1: la < LATS - 1}
+
+    def kept_in(r, x):
+        a = -1 if r < 1 else (1 if r > 8 else 0)
+        return jnp.where(inside[a], x, 0.0) if a else x
 
     for c in loads[:5]:
         c.wait()
@@ -326,17 +322,17 @@
 
     arrive(first)
     assemble(edge, [arrived[0, n].astype(F32) for n in range(6)], la > 0, la < LATS - 1)
-    clear(sx, 2, 10)
+    sx[0:2] = jnp.where(inside[-1], sx[0:2], jnp.zeros((2, COLS, CH), B16))
+    sx[10:12] = jnp.where(inside[1], sx[10:12], jnp.zeros((2, COLS, CH), B16))
     border(sx, edge, w1, False, prod)
     for r in range(10):
         y, slope[r] = silu_parts(gathered(prod, r * PITCH + 7, COLS))
-        hx[r] = y.astype(B16)
+        hx[r] = kept_in(r, y).astype(B16)
     row10 = iota((10, CH), 0)
     outside = ((row10 == 0) & (la == 0)) | ((row10 == 9) & (la == LATS - 1))
     for b in range(2):
         y, slope_side[b, 0:10] = silu_parts(columns(prod, 71 * b + 6 * (1 - b)))
         side[b, 0:10] = jnp.where(outside, 0.0, y)
-    clear(hx, 1, 9)
 
     for c in loads[7:]:
         c.wait()
@@ -384,7 +380,6 @@
         cells.append(cell)
         shares.append(w * res)
 
-    depart(qbuf, q2, back_sem, OTHERS[:FIRST])
     total = jnp.zeros((128, 256), F32)
     for t in range(0, TILES // 8, 2):
         cell = jnp.concatenate(cells[t : t + 2], axis=1)
@@ -415,8 +410,6 @@
         out4.append(((a, b), send(zs, zr.at[m], (z_sem.at[n, 0], z_sem.at[m, 1]), near(a, b))))
     each(out4, lambda c: c.start())
 
-    depart(qbuf, q2, back_sem, OTHERS[FIRST:])
-    kept = stay(qbuf, q2, 1)
     group = iota((16, 128), 1) // 32
     base = jnp.where(iota((128, CH), 0) // 64 == 0, ph.astype(F32), plow.astype(F32)).astype(B16)
     sub = iota((16, 128), 0)
@@ -442,6 +435,8 @@
     for r in range(ROWS):
         local = outer([(center, r, c) for c in range(4)])
         ax[2 + r] = (mb[r] + local).astype(B16)
+    depart(qbuf, q2, back_sem, OTHERS)
+    kept = stay(qbuf, q2, 1)
     for j in range(3):
         inner(ax, w2, True, prod, j)
 
@@ -452,7 +447,8 @@
         piece = outer([(around[a, 0], r, c) for r in rows for c in range(4)])
         for n, r in enumerate(rows):
             row = r + 2 + a * 8
-            ax[row] = (mx[row].astype(F32) + piece[n * 64 : (n + 1) * 64]).astype(B16)
+            x = mx[row].astype(F32) + piece[n * 64 : (n + 1) * 64]
+            ax[row] = jnp.where(inside[a], x, 0.0).astype(B16)
     strips = []
     for a, b in CORNERS:
         z = around[a, b]
@@ -469,20 +465,14 @@
         for n in range(6)
     ]
     assemble(edge, parts, la > 0, la < LATS - 1)
-    clear(ax, 2, 10)
 
     border(ax, edge, w2, True, prod)
     for r in range(10):
-        hx[r] = (gathered(prod, r * PITCH + 7, COLS) * slope[r]).astype(B16)
+        hx[r] = kept_in(r, gathered(prod, r * PITCH + 7, COLS) * slope[r]).astype(B16)
     for b in range(2):
         y = columns(prod, 71 * b + 6 * (1 - b)) * slope_side[b, 0:10]
         side[b, 0:10] = jnp.where(outside, 0.0, y)
-    clear(hx, 1, 9)
     products(hx, side, w1, True, prod)
-    for r in range(ROWS):
-        y = gathered(prod, r * PITCH + 7, COLS) + ax[2 + r].astype(F32)
-        grad[r] = y.astype(B16)
-
     kept.wait()
     settle(qbuf, q2, back_sem, 1)
     back = q2[:, 0, :].T[0:CAP]
@@ -491,6 +481,9 @@
     two = rest.astype(B16)
     three = (rest - two.astype(F32)).astype(B16)
     lhs = jnp.concatenate([one, two, three], axis=0)
+    for r in range(ROWS):
+        y = gathered(prod, r * PITCH + 7, COLS) + ax[2 + r].astype(F32)
+        grad[r] = y.astype(B16)
     for c in range(4):
         cut = slice(c * 512, (c + 1) * 512)
         got = jnp.dot(lhs, dt[:, cut], preferred_element_type=F32)

time: 27.4 us -> 27.3 us (level)
  no operation moved by 1% of the time
where the time goes in v8:
time: 27.3 us; the launch traced here: 27.2 us
  Pallas kernels  25.2 us (92%)
  local copies, waits for them, and re-layouts  1.3 us (5%)
  between operations  0.64 us (2%)
    pallas_call x1, Pallas kernels, on_device(): pl.pallas_call(kernel, out_shape=(pltpu.VMEM((ROWS, COLS, CH), B16), pltp...  25.2 us
    unnamed x2, local copies, waits for them, and re-layouts  1.3 us

profile of v8, /device:TPU:1, one launch (start us, length us, event | category | flops | bytes accessed | tf_op | source)
XLA Modules:
  0.0 27.2 jit_solution(17948637024119661604)
XLA Ops:
  0.6 25.2 %shard_map.113 = (bf16[8,64,256]{2,1,0:T(8,128)(2,1)S(1)}, f32[1,2048]{1,0:T(1,128)S(1)}) custom-call(s32[1,2048]{1,0:T(1,128)} %bitcast.6, s32[4,2048]{1,0:T(4,128)} %taps_in.1, f32[4,2048]{1,0:T(4,128)} %wts_in.1, f32[1,2048]{1,0:T(1,128)} %bitcast.7, f32[1,2048]{1,0:T(1,128)} %bitcast.8, f32[1,256]{1,0:T(1,128)} %bitcast.9, bf16[8,64,256]{2,1,0:T(8,128)(2,1)} %state.1, ...), custom_call_target="tpu_custom_call" | custom-call | tf_op jit(solution)/shard_map/pallas_call | solution.py:508
  25.9 0.7 %copy.14 = bf16[8,64,256]{2,1,0:T(8,128)(2,1)} copy(bf16[8,64,256]{2,1,0:T(8,128)(2,1)S(1)} %get-tuple-element.6) | data formatting | bytes 524288
  26.6 0.6 %copy.15 = f32[2048]{0:T(1024)} copy(f32[2048]{0:T(1024)S(1)} %bitcast.5) | data formatting | bytes 16384

commit v9 on v8

--- a/solution.py
+++ b/solution.py
@@ -473,26 +473,25 @@
         y = columns(prod, 71 * b + 6 * (1 - b)) * slope_side[b, 0:10]
         side[b, 0:10] = jnp.where(outside, 0.0, y)
     products(hx, side, w1, True, prod)
+    each(first + second + out4, lambda c: c.wait_send())
+    settle(sbuf, r2, out_sem, 0)
     kept.wait()
     settle(qbuf, q2, back_sem, 1)
     back = q2[:, 0, :].T[0:CAP]
     one = back.astype(B16)
     rest = back - one.astype(F32)
     two = rest.astype(B16)
-    three = (rest - two.astype(F32)).astype(B16)
-    lhs = jnp.concatenate([one, two, three], axis=0)
+    lhs = jnp.concatenate([one, two], axis=0)
     for r in range(ROWS):
         y = gathered(prod, r * PITCH + 7, COLS) + ax[2 + r].astype(F32)
         grad[r] = y.astype(B16)
     for c in range(4):
         cut = slice(c * 512, (c + 1) * 512)
         got = jnp.dot(lhs, dt[:, cut], preferred_element_type=F32)
-        got = got[0:32] + got[32:64] + got[64:96]
+        got = got[0:32] + got[32:64]
         own = iota((CAP, 512), 0) == rank_s[0:1, cut].astype(I32)
         innov[0:1, cut] = jnp.sum(jnp.where(own, got, 0.0), axis=0, keepdims=True)
 
-    each(first + second + out4, lambda c: c.wait_send())
-    settle(sbuf, r2, out_sem, 0)
     settle(qbuf, q2, back_sem, 0)
 
 

time: 27.3 us -> 27.2 us (level)
  no operation moved by 1% of the time
where the time goes in v9:
time: 27.2 us; the launch traced here: 27.1 us
  Pallas kernels  25.1 us (92%)
  local copies, waits for them, and re-layouts  1.3 us (5%)
  between operations  0.64 us (2%)
    pallas_call x1, Pallas kernels, on_device(): pl.pallas_call(kernel, out_shape=(pltpu.VMEM((ROWS, COLS, CH), B16), pltp...  25.1 us
    unnamed x2, local copies, waits for them, and re-layouts  1.3 us

profile of v9, /device:TPU:1, one launch (start us, length us, event | category | flops | bytes accessed | tf_op | source)
XLA Modules:
  0.0 27.1 jit_solution(18276474841739757307)
XLA Ops:
  0.6 25.1 %shard_map.113 = (bf16[8,64,256]{2,1,0:T(8,128)(2,1)S(1)}, f32[1,2048]{1,0:T(1,128)S(1)}) custom-call(s32[1,2048]{1,0:T(1,128)} %bitcast.6, s32[4,2048]{1,0:T(4,128)} %taps_in.1, f32[4,2048]{1,0:T(4,128)} %wts_in.1, f32[1,2048]{1,0:T(1,128)} %bitcast.7, f32[1,2048]{1,0:T(1,128)} %bitcast.8, f32[1,256]{1,0:T(1,128)} %bitcast.9, bf16[8,64,256]{2,1,0:T(8,128)(2,1)} %state.1, ...), custom_call_target="tpu_custom_call" | custom-call | tf_op jit(solution)/shard_map/pallas_call | solution.py:507
  25.8 0.7 %copy.14 = bf16[8,64,256]{2,1,0:T(8,128)(2,1)} copy(bf16[8,64,256]{2,1,0:T(8,128)(2,1)S(1)} %get-tuple-element.6) | data formatting | bytes 524288
  26.5 0.6 %copy.15 = f32[2048]{0:T(1024)} copy(f32[2048]{0:T(1024)S(1)} %bitcast.5) | data formatting | bytes 16384
